TPU v7x, 256 devices: a whole 4x4x8 slice. The times are simulated.
256 devices in a mesh: owner: 128 (over z, y, x), ens: 2 (over core).
Axes of the slice: x: 4, y: 4, z: 8, core: 2. Of those that a mesh axis runs over, the one named last changes fastest.
Arguments:
- noisy_state: bfloat16 [4, 12, 8192, 128], P('ens', None, 'owner'), may hold values from -6 to 6
- condition: bfloat16 [12, 8192, 128], P(None, 'owner'), may hold values from -6 to 6
- counts: int32 [128], P('owner'), may hold values from 1 to 4, as said below
- offsets: int32 [128], P('owner'), may hold values from 0 to 64
- conv_in_weight: bfloat16 [3, 3, 24, 128], replicated, may hold values from -0.4375 to 0.4375
- conv_mid_weight: bfloat16 [3, 3, 128, 128], replicated, may hold values from -0.1875 to 0.1875
- proj_out_weight: bfloat16 [12, 128], replicated, may hold values from -0.5 to 0.5
- modulation: float32 [2, 128], replicated, may hold values from -3 to 3
Outputs:
- next_state: float32 [4, 12, 8192, 128], P('ens', None, 'owner')
Inputs may be any that keep to these rules, and one draw needn't show every extreme that they name: `counts`: some tile runs all 4 members in every draw.
All inputs are finite; a program needn't handle non-finite values.
Results may differ from a plain program's by a relative error of at most 0.00032.
Values may be sent and summed in bfloat16 or wider, within the bound.
A program may use at most 320 MiB of HBM per device.

v0:
```python
import math

import jax
import jax.numpy as jnp
from jax import lax
from jax.sharding import PartitionSpec as P

GROUPS = 32


sigma_now = 2.0
sigma_next = 1.0
sigma_data = 0.5
input_scale = 1.0 / math.sqrt(sigma_now**2 + sigma_data**2)
skip_scale = sigma_data**2 / (sigma_now**2 + sigma_data**2)
output_scale = sigma_now * sigma_data / math.sqrt(sigma_now**2 + sigma_data**2)
step_factor = (sigma_next - sigma_now) / sigma_now
norm_epsilon = 1e-05


def padded_2(block, sides, width):
    for axis, dim in sides:
        count = lax.axis_size(axis)
        forward = [(i, i + 1) for i in range(count - 1)]
        forward.append((count - 1, 0))
        backward = [(target, source) for source, target in forward]
        low = lax.ppermute(
            lax.slice_in_dim(block, block.shape[dim] - width, None, axis=dim), axis, forward
        )
        high = lax.ppermute(lax.slice_in_dim(block, 0, width, axis=dim), axis, backward)
        block = jnp.concatenate([low, block, high], axis=dim)
    return block


def shifted(x, axis, by):
    length = lax.axis_size(axis)
    return lax.ppermute(x, axis, [(i, (i + by) % length) for i in range(length)])


def blend_weights(length_cells):
    places = jnp.arange(length_cells).astype(jnp.float32)
    return 0.1 + jnp.sin(math.pi * (places + 0.5) / length_cells) ** 2


def group_norm(values, groups):
    channels, columns, row_count = values.shape
    grouped = values.reshape(groups, channels // groups, columns, row_count)
    center = jnp.mean(grouped, axis=(1, 2, 3), keepdims=True)
    spread = jnp.mean(jnp.square(grouped - center), axis=(1, 2, 3), keepdims=True)
    return ((grouped - center) / jnp.sqrt(spread + norm_epsilon)).reshape(
        channels, columns, row_count
    )


def convolve(values, kernel):
    columns, row_count = (values.shape[1], values.shape[2])
    padded = jnp.pad(values, ((0, 0), (1, 1), (1, 1)))
    stacked_taps = jnp.stack(
        [
            padded[:, across : across + columns, downward : downward + row_count]
            for across in range(3)
            for downward in range(3)
        ],
        axis=0,
    )
    flat_kernel = kernel.reshape(9, kernel.shape[2], kernel.shape[3])
    return jnp.einsum(
        "kcxy,kcf->fxy", stacked_taps, flat_kernel, preferred_element_type=jnp.float32
    )


def member_update(
    noisy_tile, context, conv_in_weight, conv_mid_weight, proj_out_weight, modulation
):
    noisy_float = noisy_tile.astype(jnp.float32)
    scaled = (input_scale * noisy_float).astype(jnp.bfloat16)
    first_conv = convolve(jnp.concatenate([scaled, context], axis=0), conv_in_weight)
    modulated = (
        group_norm(first_conv, GROUPS) * (1.0 + modulation[0][:, None, None])
        + modulation[1][:, None, None]
    )
    hidden = jax.nn.silu(modulated).astype(jnp.bfloat16)
    second = convolve(hidden, conv_mid_weight)
    mixed_out = jax.nn.silu(group_norm(first_conv + second, GROUPS)).astype(jnp.bfloat16)
    output = jnp.einsum(
        "fxy,cf->cxy", mixed_out, proj_out_weight, preferred_element_type=jnp.float32
    )
    denoised = skip_scale * noisy_float + output_scale * output
    return step_factor * (noisy_float - denoised)


def on_device(
    noisy_state,
    condition,
    counts,
    offsets,
    conv_in_weight,
    conv_mid_weight,
    proj_out_weight,
    modulation,
):
    slot_count, channels, block_width, row_count = noisy_state.shape
    tile_span = 2 * block_width
    core_index = lax.axis_index("ens")
    noisy_all = padded_2(noisy_state, (("owner", 2),), block_width)
    context_all = padded_2(condition, (("owner", 1),), block_width)
    shift_cols = offsets[0]
    tile_count = counts[0]
    noisy_tiles = lax.dynamic_slice_in_dim(noisy_all, shift_cols, tile_span, 2)
    context_tile = lax.dynamic_slice_in_dim(context_all, shift_cols, tile_span, 1)
    blending = blend_weights(tile_span)
    weight_canvas = lax.dynamic_update_slice_in_dim(
        jnp.zeros((3 * block_width,), jnp.float32), blending, shift_cols, 0
    )

    def weighted_update(slot_noisy):
        update = member_update(
            slot_noisy, context_tile, conv_in_weight, conv_mid_weight, proj_out_weight, modulation
        )
        return blending[None, :, None] * update

    def slot_canvas(slot_noisy, member_index):
        member_term = jnp.where(member_index < tile_count, weighted_update(slot_noisy), 0.0)
        empty_canvas = jnp.zeros((channels, 3 * block_width, row_count), jnp.float32)
        return lax.dynamic_update_slice_in_dim(empty_canvas, member_term, shift_cols, 1)

    member_ids = core_index * slot_count + jnp.arange(slot_count, dtype=jnp.int32)
    canvas = lax.map(
        lambda member_pair: slot_canvas(member_pair[0], member_pair[1]), (noisy_tiles, member_ids)
    )
    from_right = shifted((canvas[:, :, :block_width], weight_canvas[:block_width]), "owner", -1)
    from_left = shifted(
        (canvas[:, :, 2 * block_width :], weight_canvas[2 * block_width :]), "owner", 1
    )
    numerator = canvas[:, :, block_width : 2 * block_width] + from_right[0] + from_left[0]
    weights = weight_canvas[block_width : 2 * block_width] + from_right[1] + from_left[1]
    return noisy_state.astype(jnp.float32) + numerator / weights[None, None, :, None]


def solution(mesh):
    placed = (
        P("ens", None, "owner", None),
        P(None, "owner", None),
        P("owner"),
        P("owner"),
        P(),
        P(),
        P(),
        P(),
    )
    return jax.shard_map(
        on_device,
        mesh=mesh,
        in_specs=placed,
        out_specs=P("ens", None, "owner", None),
        check_vma=False,
    )
```

profile of v0, /device:TPU:1, one launch (start us, length us, event | category | flops | bytes accessed | tf_op | source)
XLA Modules:
  0.0 282.4 jit_solution(388361780014954592)
XLA Ops:
  3.4 9.1 %collective-permute-start.1 = (bf16[2,12,64,128]{3,1,2,0:T(8,128)(2,1)S(1)}, bf16[2,12,64,128]{3,1,2,0:T(8,128)(2,1)S(1)}, u32[]{:S(2)}, u32[]{:S(2)}) collective-permute-start(bf16[2,12,64,128]{3,1,2,0:T(8,128)(2,1)S(1)} %copy.38), channel_id=1, source_target_pairs={{2,0},{4,2},{6,4},{8,6},{10,8},{12,10},{14,12},{16,14},{18,16},{20... | collective-permute-start | bytes 1179656 | tf_op jit(solution)/shard_map/ppermute | solution.py:30
  13.6 6.9 %collective-permute-start.3 = (bf16[12,64,128]{2,0,1:T(8,128)(2,1)S(1)}, bf16[12,64,128]{2,0,1:T(8,128)(2,1)S(1)}, u32[]{:S(2)}, u32[]{:S(2)}) collective-permute-start(bf16[12,64,128]{2,0,1:T(8,128)(2,1)S(1)} %copy.41), channel_id=1, source_target_pairs={{2,0},{4,2},{6,4},{8,6},{10,8},{12,10},{14,12},{16,14},{18,16},{20... | collective-permute-start | bytes 589832 | tf_op jit(solution)/shard_map/ppermute | solution.py:30
  21.2 8.5 %collective-permute-done.2 = bf16[12,64,128]{2,0,1:T(8,128)(2,1)S(1)} collective-permute-done((bf16[12,64,128]{2,0,1:T(8,128)(2,1)S(1)}, bf16[12,64,128]{2,0,1:T(8,128)(2,1)S(1)}, u32[]{:S(2)}, u32[]{:S(2)}) %collective-permute-start.2) | collective-permute-done | bytes 196640 | tf_op jit(solution)/shard_map/ppermute | solution.py:27
  32.6 216.4 %while.13 = (s32[]{:T(128)}, f32[2,12,192,128]{3,2,1,0:T(8,128)}, s32[2]{0:T(128)S(1)}, s32[]{:T(128)}, bf16[2,12,128,128]{3,1,2,0:T(8,128)(2,1)S(1)}, /*index=5...) while((s32[]{:T(128)}, f32[2,12,192,128]{3,2,1,0:T(8,128)}, ...), condition=%wide.region_9.10_spmd.clone, body=%wide.region_0.9_spmd.clone.sunk | while | flops 5862982656 | bytes 236023664 | solution.py:128
  59.7 7.2 %bitcast_reduce_fusion.2 = (f32[128]{0:T(128)S(1)}, f32[128,128,128,1]{2,1,3,0:T(8,128)}) fusion(bf16[9,24,128,128]{3,1,0,2:T(8,128)(2,1)S(1)} %fusion.97, bf16[9,24,128,1]{2,1,0,3:T(8,128)(2,1)S(1)} %bitcast.252), kind=kOutput, calls=%fused_computation.13.clone.1 | convolution fusion | flops 908066688 | bytes 15522304 | tf_op jit(solution)/shard_map/while/body/eval_jaxpr/kcxy,kcf->fxy/dot_general | solution.py:67
  67.3 5.6 %multiply_reduce_fusion.4 = f32[128]{0:T(128)S(1)} fusion(f32[128,128,128,1]{2,1,3,0:T(8,128)} %get-tuple-element.288, f32[128]{0:T(128)S(1)} %sub.148), kind=kLoop, calls=%fused_computation.15.clone.1 | loop fusion | flops 6291328 | bytes 8389632 | tf_op jit(solution)/shard_map/while/body/eval_jaxpr/reduce_sum | solution.py:49
  73.3 5.0 %fusion.98 = bf16[128,128,128]{0,2,1:T(8,128)(2,1)S(1)} fusion(f32[128,128,128,1]{2,1,3,0:T(8,128)} %get-tuple-element.288, f32[128]{0:T(128)S(1)} %get-tuple-element.289, f32[128]{0:T(128)S(1)} %get-tuple-element.290, f32[128]{0:T(128)S(1)} %div.226, f32[128]{0:T(128)S(1)} %sub.148), kind=kLoop, calls=%fused_computation.16.clone.2 | loop fusion | flops 18874368 | bytes 12584960 | tf_op jit(solution)/shard_map/while/body/eval_jaxpr/convert_element_type | solution.py:82
  84.2 4.6 %bitcast_dynamic-update-slice_fusion.23 = bf16[9,128,128,128]{1,3,2,0:T(8,128)(2,1)} fusion(bf16[9,128,128,128]{1,3,2,0:T(8,128)(2,1)} %bitcast_dynamic-update-slice_fusion.22, bf16[128,128,128]{0,2,1:T(8,128)(2,1)S(1)} %fusion.98), kind=kLoop, calls=%fused_computation.24.clone.1 | loop fusion | bytes 8388608 | tf_op jit(solution)/shard_map/while
  88.8 4.4 %bitcast_dynamic-update-slice_fusion.24 = bf16[9,128,128,128]{1,3,2,0:T(8,128)(2,1)} fusion(bf16[9,128,128,128]{1,3,2,0:T(8,128)(2,1)} %bitcast_dynamic-update-slice_fusion.23, bf16[128,128,128]{0,2,1:T(8,128)(2,1)S(1)} %fusion.98), kind=kLoop, calls=%fused_computation.23.clone.1 | loop fusion | bytes 8388608 | tf_op jit(solution)/shard_map/while
  93.2 4.0 %bitcast_dynamic-update-slice_fusion.25 = bf16[9,128,128,128]{1,3,2,0:T(8,128)(2,1)} fusion(bf16[9,128,128,128]{1,3,2,0:T(8,128)(2,1)} %bitcast_dynamic-update-slice_fusion.24, f32[128]{0:T(128)S(1)} %get-tuple-element.289, f32[128]{0:T(128)S(1)} %get-tuple-element.290, f32[128]{0:T(128)S(1)} %div.226, f32[128]{0:T(128)S(1)} %sub.148, ...), kind=kLoop, calls=%fused_computation.22.clone.1 | loop fusion | flops 18874368 | bytes 12584960 | tf_op jit(solution)/shard_map/while
  97.2 4.8 %bitcast_dynamic-update-slice_fusion.26 = bf16[9,128,128,128]{1,3,2,0:T(8,128)(2,1)} fusion(bf16[9,128,128,128]{1,3,2,0:T(8,128)(2,1)} %bitcast_dynamic-update-slice_fusion.25, bf16[128,128,128]{0,2,1:T(8,128)(2,1)S(1)} %fusion.98), kind=kLoop, calls=%fused_computation.21.clone.1 | loop fusion | bytes 8388608 | tf_op jit(solution)/shard_map/while
  102.0 4.5 %bitcast_dynamic-update-slice_fusion.27 = bf16[9,128,128,128]{1,3,2,0:T(8,128)(2,1)} fusion(bf16[9,128,128,128]{1,3,2,0:T(8,128)(2,1)} %bitcast_dynamic-update-slice_fusion.26, bf16[128,128,128]{0,2,1:T(8,128)(2,1)S(1)} %fusion.98), kind=kLoop, calls=%fused_computation.20.clone.1 | loop fusion | bytes 8388608 | tf_op jit(solution)/shard_map/while
  109.0 4.8 %bitcast_dynamic-update-slice_fusion.29 = bf16[9,128,128,128]{1,3,2,0:T(8,128)(2,1)} fusion(bf16[9,128,128,128]{1,3,2,0:T(8,128)(2,1)} %bitcast_dynamic-update-slice_fusion.28, bf16[128,128,128]{0,2,1:T(8,128)(2,1)S(1)} %fusion.98), kind=kLoop, calls=%fused_computation.18.clone.1 | loop fusion | bytes 8388608 | tf_op jit(solution)/shard_map/while/body/eval_jaxpr/stack | solution.py:58
  113.8 22.5 %fusion.99 = (f32[128]{0:T(128)S(1)}, f32[128,128,128]{2,1,0:T(8,128)}) fusion(bf16[9,128,128,128]{1,3,2,0:T(8,128)(2,1)} %bitcast_dynamic-update-slice_fusion.29, bf16[9,128,128,1]{2,1,3,0:T(8,128)(2,1)S(1)} %bitcast.251, f32[128,128,128,1]{2,1,3,0:T(8,128)} %get-tuple-element.288), kind=kOutput, calls=%fused_computation.89.clone.1 | convolution fusion | flops 4836032512 | bytes 54821376 | tf_op jit(solution)/shard_map/while/body/eval_jaxpr/kcxy,kcf->fxy/dot_general | solution.py:67
  136.8 5.6 %multiply_reduce_fusion.5 = f32[128]{0:T(128)S(1)} fusion(f32[128,128,128]{2,1,0:T(8,128)} %get-tuple-element.292, f32[128]{0:T(128)S(1)} %sub.150), kind=kLoop, calls=%fused_computation.14.clone.1 | loop fusion | flops 6291328 | bytes 8389632 | tf_op jit(solution)/shard_map/while/body/eval_jaxpr/reduce_sum | solution.py:49
  144.9 4.8 %fusion.100 = f32[1,12,192,128]{3,1,2,0:T(8,128)S(1)} fusion(f32[1,12,192,128]{3,1,2,0:T(8,128)S(1)} %broadcast_in_dim.34, s32[]{:T(128)} %get-tuple-element.330, f32[128,128,128]{2,1,0:T(8,128)} %get-tuple-element.292, f32[128]{0:T(128)S(1)} %div.228, f32[128]{0:T(128)S(1)} %sub.150, f32[128]{0:T(128)S(1)} %add_multiply_fusion.2, pred[]{:T(512)S(6)} %lt.24, ...), kind=kOutput, calls=%fused_computation.45.clone.1 | convolution fusion | flops 66387968 | bytes 9967113 | tf_op jit(solution)/shard_map/while/body/eval_jaxpr/fxy,cf->cxy/dot_general | solution.py:85
  154.4 7.2 %bitcast_reduce_fusion.2 = (f32[128]{0:T(128)S(1)}, f32[128,128,128,1]{2,1,3,0:T(8,128)}) fusion(bf16[9,24,128,128]{3,1,0,2:T(8,128)(2,1)S(1)} %fusion.97, bf16[9,24,128,1]{2,1,0,3:T(8,128)(2,1)S(1)} %bitcast.252), kind=kOutput, calls=%fused_computation.13.clone.1 | convolution fusion | flops 908066688 | bytes 15522304 | tf_op jit(solution)/shard_map/while/body/eval_jaxpr/kcxy,kcf->fxy/dot_general | solution.py:67
  161.9 5.6 %multiply_reduce_fusion.4 = f32[128]{0:T(128)S(1)} fusion(f32[128,128,128,1]{2,1,3,0:T(8,128)} %get-tuple-element.288, f32[128]{0:T(128)S(1)} %sub.148), kind=kLoop, calls=%fused_computation.15.clone.1 | loop fusion | flops 6291328 | bytes 8389632 | tf_op jit(solution)/shard_map/while/body/eval_jaxpr/reduce_sum | solution.py:49
  168.0 5.0 %fusion.98 = bf16[128,128,128]{0,2,1:T(8,128)(2,1)S(1)} fusion(f32[128,128,128,1]{2,1,3,0:T(8,128)} %get-tuple-element.288, f32[128]{0:T(128)S(1)} %get-tuple-element.289, f32[128]{0:T(128)S(1)} %get-tuple-element.290, f32[128]{0:T(128)S(1)} %div.226, f32[128]{0:T(128)S(1)} %sub.148), kind=kLoop, calls=%fused_computation.16.clone.2 | loop fusion | flops 18874368 | bytes 12584960 | tf_op jit(solution)/shard_map/while/body/eval_jaxpr/convert_element_type | solution.py:82
  178.9 4.6 %bitcast_dynamic-update-slice_fusion.23 = bf16[9,128,128,128]{1,3,2,0:T(8,128)(2,1)} fusion(bf16[9,128,128,128]{1,3,2,0:T(8,128)(2,1)} %bitcast_dynamic-update-slice_fusion.22, bf16[128,128,128]{0,2,1:T(8,128)(2,1)S(1)} %fusion.98), kind=kLoop, calls=%fused_computation.24.clone.1 | loop fusion | bytes 8388608 | tf_op jit(solution)/shard_map/while
  183.5 4.4 %bitcast_dynamic-update-slice_fusion.24 = bf16[9,128,128,128]{1,3,2,0:T(8,128)(2,1)} fusion(bf16[9,128,128,128]{1,3,2,0:T(8,128)(2,1)} %bitcast_dynamic-update-slice_fusion.23, bf16[128,128,128]{0,2,1:T(8,128)(2,1)S(1)} %fusion.98), kind=kLoop, calls=%fused_computation.23.clone.1 | loop fusion | bytes 8388608 | tf_op jit(solution)/shard_map/while
  187.9 4.0 %bitcast_dynamic-update-slice_fusion.25 = bf16[9,128,128,128]{1,3,2,0:T(8,128)(2,1)} fusion(bf16[9,128,128,128]{1,3,2,0:T(8,128)(2,1)} %bitcast_dynamic-update-slice_fusion.24, f32[128]{0:T(128)S(1)} %get-tuple-element.289, f32[128]{0:T(128)S(1)} %get-tuple-element.290, f32[128]{0:T(128)S(1)} %div.226, f32[128]{0:T(128)S(1)} %sub.148, ...), kind=kLoop, calls=%fused_computation.22.clone.1 | loop fusion | flops 18874368 | bytes 12584960 | tf_op jit(solution)/shard_map/while
  191.9 4.8 %bitcast_dynamic-update-slice_fusion.26 = bf16[9,128,128,128]{1,3,2,0:T(8,128)(2,1)} fusion(bf16[9,128,128,128]{1,3,2,0:T(8,128)(2,1)} %bitcast_dynamic-update-slice_fusion.25, bf16[128,128,128]{0,2,1:T(8,128)(2,1)S(1)} %fusion.98), kind=kLoop, calls=%fused_computation.21.clone.1 | loop fusion | bytes 8388608 | tf_op jit(solution)/shard_map/while
  196.7 4.5 %bitcast_dynamic-update-slice_fusion.27 = bf16[9,128,128,128]{1,3,2,0:T(8,128)(2,1)} fusion(bf16[9,128,128,128]{1,3,2,0:T(8,128)(2,1)} %bitcast_dynamic-update-slice_fusion.26, bf16[128,128,128]{0,2,1:T(8,128)(2,1)S(1)} %fusion.98), kind=kLoop, calls=%fused_computation.20.clone.1 | loop fusion | bytes 8388608 | tf_op jit(solution)/shard_map/while
  203.7 4.8 %bitcast_dynamic-update-slice_fusion.29 = bf16[9,128,128,128]{1,3,2,0:T(8,128)(2,1)} fusion(bf16[9,128,128,128]{1,3,2,0:T(8,128)(2,1)} %bitcast_dynamic-update-slice_fusion.28, bf16[128,128,128]{0,2,1:T(8,128)(2,1)S(1)} %fusion.98), kind=kLoop, calls=%fused_computation.18.clone.1 | loop fusion | bytes 8388608 | tf_op jit(solution)/shard_map/while/body/eval_jaxpr/stack | solution.py:58
  208.5 22.5 %fusion.99 = (f32[128]{0:T(128)S(1)}, f32[128,128,128]{2,1,0:T(8,128)}) fusion(bf16[9,128,128,128]{1,3,2,0:T(8,128)(2,1)} %bitcast_dynamic-update-slice_fusion.29, bf16[9,128,128,1]{2,1,3,0:T(8,128)(2,1)S(1)} %bitcast.251, f32[128,128,128,1]{2,1,3,0:T(8,128)} %get-tuple-element.288), kind=kOutput, calls=%fused_computation.89.clone.1 | convolution fusion | flops 4836032512 | bytes 54821376 | tf_op jit(solution)/shard_map/while/body/eval_jaxpr/kcxy,kcf->fxy/dot_general | solution.py:67
  231.4 5.6 %multiply_reduce_fusion.5 = f32[128]{0:T(128)S(1)} fusion(f32[128,128,128]{2,1,0:T(8,128)} %get-tuple-element.292, f32[128]{0:T(128)S(1)} %sub.150), kind=kLoop, calls=%fused_computation.14.clone.1 | loop fusion | flops 6291328 | bytes 8389632 | tf_op jit(solution)/shard_map/while/body/eval_jaxpr/reduce_sum | solution.py:49
  239.6 4.8 %fusion.100 = f32[1,12,192,128]{3,1,2,0:T(8,128)S(1)} fusion(f32[1,12,192,128]{3,1,2,0:T(8,128)S(1)} %broadcast_in_dim.34, s32[]{:T(128)} %get-tuple-element.330, f32[128,128,128]{2,1,0:T(8,128)} %get-tuple-element.292, f32[128]{0:T(128)S(1)} %div.228, f32[128]{0:T(128)S(1)} %sub.150, f32[128]{0:T(128)S(1)} %add_multiply_fusion.2, pred[]{:T(512)S(6)} %lt.24, ...), kind=kOutput, calls=%fused_computation.45.clone.1 | convolution fusion | flops 66387968 | bytes 9967113 | tf_op jit(solution)/shard_map/while/body/eval_jaxpr/fxy,cf->cxy/dot_general | solution.py:85
  250.4 6.7 %collective-permute-start.4 = (f32[2,12,64,128]{3,2,1,0:T(8,128)S(1)}, f32[2,12,64,128]{3,2,1,0:T(8,128)S(1)}, u32[]{:S(2)}, u32[]{:S(2)}) collective-permute-start(f32[2,12,64,128]{3,2,1,0:T(8,128)S(1)} %get-tuple-element.211), channel_id=1, source_target_pairs={{0,254},{2,0},{4,2},{6,4},{8,6},{10,8},{12,10},{14,12},{16,14},{18... | collective-permute-start | bytes 2359304 | tf_op jit(solution)/shard_map/ppermute | solution.py:37
  257.3 6.9 %collective-permute-start.6 = (f32[64]{0:T(128)S(1)}, f32[64]{0:T(128)S(1)}, u32[]{:S(2)}, u32[]{:S(2)}) collective-permute-start(f32[64]{0:T(128)S(1)} %get-tuple-element.213), channel_id=1, source_target_pairs={{0,254},{2,0},{4,2},{6,4},{8,6},{10,8},{12,10},{14,12},{16,14},{18... | collective-permute-start | bytes 776 | tf_op jit(solution)/shard_map/ppermute | solution.py:37
  264.2 8.3 %collective-permute-done.6 = f32[64]{0:T(128)S(1)} collective-permute-done((f32[64]{0:T(128)S(1)}, f32[64]{0:T(128)S(1)}, u32[]{:S(2)}, u32[]{:S(2)}) %collective-permute-start.6) | collective-permute-done | bytes 288 | tf_op jit(solution)/shard_map/ppermute | solution.py:37
  272.5 7.3 %collective-permute-done.7 = f32[64]{0:T(128)S(1)} collective-permute-done((f32[64]{0:T(128)S(1)}, f32[64]{0:T(128)S(1)}, u32[]{:S(2)}, u32[]{:S(2)}) %collective-permute-start.7) | collective-permute-done | bytes 288 | tf_op jit(solution)/shard_map/ppermute | solution.py:37
  (127 shorter events, 42.3 us)
Async XLA Ops:
  1.3 29.6 %collective-permute-start = (bf16[2,12,64,128]{3,1,2,0:T(8,128)(2,1)S(1)}, bf16[2,12,64,128]{3,1,2,0:T(8,128)(2,1)S(1)}, u32[]{:S(2)}, u32[]{:S(2)}) collective-permute-start(bf16[2,12,64,128]{3,1,2,0:T(8,128)(2,1)S(1)} %copy.38), channel_id=1, source_target_pairs={{0,2},{2,4},{4,6},{6,8},{8,10},{10,12},{12,14},{14,16},{16,18},{18... | collective-permute-start | bytes 1179656 | tf_op jit(solution)/shard_map/ppermute | solution.py:27
  3.4 27.5 %collective-permute-start.1 = (bf16[2,12,64,128]{3,1,2,0:T(8,128)(2,1)S(1)}, bf16[2,12,64,128]{3,1,2,0:T(8,128)(2,1)S(1)}, u32[]{:S(2)}, u32[]{:S(2)}) collective-permute-start(bf16[2,12,64,128]{3,1,2,0:T(8,128)(2,1)S(1)} %copy.38), channel_id=1, source_target_pairs={{2,0},{4,2},{6,4},{8,6},{10,8},{12,10},{14,12},{16,14},{18,16},{20... | collective-permute-start | bytes 1179656 | tf_op jit(solution)/shard_map/ppermute | solution.py:30
  13.6 16.1 %collective-permute-start.2 = (bf16[12,64,128]{2,0,1:T(8,128)(2,1)S(1)}, bf16[12,64,128]{2,0,1:T(8,128)(2,1)S(1)}, u32[]{:S(2)}, u32[]{:S(2)}) collective-permute-start(bf16[12,64,128]{2,0,1:T(8,128)(2,1)S(1)} %copy.41), channel_id=1, source_target_pairs={{0,2},{2,4},{4,6},{6,8},{8,10},{10,12},{12,14},{14,16},{16,18},{18... | collective-permute-start | bytes 589832 | tf_op jit(solution)/shard_map/ppermute | solution.py:27
  13.6 16.0 %collective-permute-start.3 = (bf16[12,64,128]{2,0,1:T(8,128)(2,1)S(1)}, bf16[12,64,128]{2,0,1:T(8,128)(2,1)S(1)}, u32[]{:S(2)}, u32[]{:S(2)}) collective-permute-start(bf16[12,64,128]{2,0,1:T(8,128)(2,1)S(1)} %copy.41), channel_id=1, source_target_pairs={{2,0},{4,2},{6,4},{8,6},{10,8},{12,10},{14,12},{16,14},{18,16},{20... | collective-permute-start | bytes 589832 | tf_op jit(solution)/shard_map/ppermute | solution.py:30
  32.6 247.3 %copy-start.1 = (bf16[2,12,64,128]{3,2,1,0:T(8,128)(2,1)S(1)}, bf16[2,12,64,128]{3,2,1,0:T(8,128)(2,1)}, u32[]{:S(2)}) copy-start(bf16[2,12,64,128]{3,2,1,0:T(8,128)(2,1)} %param.10) | copy-start | bytes 1179652
  56.9 2.8 copy-start.3
  66.8 6.4 %copy-start.2 = (f32[2,128]{1,0:T(2,128)S(1)}, f32[2,128]{1,0:T(2,128)}, u32[]{:S(2)}) copy-start(f32[2,128]{1,0:T(2,128)} %get-tuple-element.327) | copy-start | bytes 3076 | tf_op jit(solution)/shard_map/while
  84.2 8.9 %slice-start = ((s8[8388608]{0:T(1024)(128)(4,1)}), s8[4194304]{0:T(1024)(128)(4,1)S(1)}, s32[]{:S(2)}) async-start(s8[8388608]{0:T(1024)(128)(4,1)} %bitcast.249), calls=%async_computation | async-start | bytes 8388608 | tf_op jit(solution)/shard_map/while
  88.8 4.4 %slice-start.1 = ((s8[8388608]{0:T(1024)(128)(4,1)}), s8[4194304]{0:T(1024)(128)(4,1)S(1)}, s32[]{:S(2)}) async-start(s8[8388608]{0:T(1024)(128)(4,1)} %bitcast.249), calls=%async_computation.1 | async-start | bytes 8388608 | tf_op jit(solution)/shard_map/while
  106.5 7.3 %copy-start = (bf16[3,3,128,128]{3,2,1,0:T(8,128)(2,1)S(1)}, bf16[3,3,128,128]{3,2,1,0:T(8,128)(2,1)}, u32[]{:S(2)}) copy-start(bf16[3,3,128,128]{3,2,1,0:T(8,128)(2,1)} %get-tuple-element.328) | copy-start | bytes 884740 | tf_op jit(solution)/shard_map/while
  136.3 8.6 %copy-start.4 = (bf16[12,128]{1,0:T(8,128)(2,1)S(1)}, bf16[12,128]{1,0:T(8,128)(2,1)}, u32[]{:S(2)}) copy-start(bf16[12,128]{1,0:T(8,128)(2,1)} %get-tuple-element.329) | copy-start | bytes 9220 | tf_op jit(solution)/shard_map/while
  151.5 2.8 copy-start.3
  161.5 6.4 %copy-start.2 = (f32[2,128]{1,0:T(2,128)S(1)}, f32[2,128]{1,0:T(2,128)}, u32[]{:S(2)}) copy-start(f32[2,128]{1,0:T(2,128)} %get-tuple-element.327) | copy-start | bytes 3076 | tf_op jit(solution)/shard_map/while
  178.9 8.9 %slice-start = ((s8[8388608]{0:T(1024)(128)(4,1)}), s8[4194304]{0:T(1024)(128)(4,1)S(1)}, s32[]{:S(2)}) async-start(s8[8388608]{0:T(1024)(128)(4,1)} %bitcast.249), calls=%async_computation | async-start | bytes 8388608 | tf_op jit(solution)/shard_map/while
  183.5 4.4 %slice-start.1 = ((s8[8388608]{0:T(1024)(128)(4,1)}), s8[4194304]{0:T(1024)(128)(4,1)S(1)}, s32[]{:S(2)}) async-start(s8[8388608]{0:T(1024)(128)(4,1)} %bitcast.249), calls=%async_computation.1 | async-start | bytes 8388608 | tf_op jit(solution)/shard_map/while
  201.2 7.3 %copy-start = (bf16[3,3,128,128]{3,2,1,0:T(8,128)(2,1)S(1)}, bf16[3,3,128,128]{3,2,1,0:T(8,128)(2,1)}, u32[]{:S(2)}) copy-start(bf16[3,3,128,128]{3,2,1,0:T(8,128)(2,1)} %get-tuple-element.328) | copy-start | bytes 884740 | tf_op jit(solution)/shard_map/while
  231.0 8.6 %copy-start.4 = (bf16[12,128]{1,0:T(8,128)(2,1)S(1)}, bf16[12,128]{1,0:T(8,128)(2,1)}, u32[]{:S(2)}) copy-start(bf16[12,128]{1,0:T(8,128)(2,1)} %get-tuple-element.329) | copy-start | bytes 9220 | tf_op jit(solution)/shard_map/while
  250.4 29.4 %collective-permute-start.4 = (f32[2,12,64,128]{3,2,1,0:T(8,128)S(1)}, f32[2,12,64,128]{3,2,1,0:T(8,128)S(1)}, u32[]{:S(2)}, u32[]{:S(2)}) collective-permute-start(f32[2,12,64,128]{3,2,1,0:T(8,128)S(1)} %get-tuple-element.211), channel_id=1, source_target_pairs={{0,254},{2,0},{4,2},{6,4},{8,6},{10,8},{12,10},{14,12},{16,14},{18... | collective-permute-start | bytes 2359304 | tf_op jit(solution)/shard_map/ppermute | solution.py:37
  257.2 22.7 %collective-permute-start.5 = (f32[2,12,64,128]{3,2,1,0:T(8,128)S(1)}, f32[2,12,64,128]{3,2,1,0:T(8,128)S(1)}, u32[]{:S(2)}, u32[]{:S(2)}) collective-permute-start(f32[2,12,64,128]{3,2,1,0:T(8,128)S(1)} %get-tuple-element.212), channel_id=1, source_target_pairs={{0,2},{2,4},{4,6},{6,8},{8,10},{10,12},{12,14},{14,16},{16,18},{18... | collective-permute-start | bytes 2359304 | tf_op jit(solution)/shard_map/ppermute | solution.py:37
  257.3 15.2 %collective-permute-start.6 = (f32[64]{0:T(128)S(1)}, f32[64]{0:T(128)S(1)}, u32[]{:S(2)}, u32[]{:S(2)}) collective-permute-start(f32[64]{0:T(128)S(1)} %get-tuple-element.213), channel_id=1, source_target_pairs={{0,254},{2,0},{4,2},{6,4},{8,6},{10,8},{12,10},{14,12},{16,14},{18... | collective-permute-start | bytes 776 | tf_op jit(solution)/shard_map/ppermute | solution.py:37
  264.2 15.6 %collective-permute-start.7 = (f32[64]{0:T(128)S(1)}, f32[64]{0:T(128)S(1)}, u32[]{:S(2)}, u32[]{:S(2)}) collective-permute-start(f32[64]{0:T(128)S(1)} %get-tuple-element.214), channel_id=1, source_target_pairs={{0,2},{2,4},{4,6},{6,8},{8,10},{10,12},{12,14},{14,16},{16,18},{18... | collective-permute-start | bytes 776 | tf_op jit(solution)/shard_map/ppermute | solution.py:37
where the time goes:
time: 288 us; the launch traced here: 282 us
  local copies, waits for them, and re-layouts  78.9 us (27%)
  matrix products  69 us (24%)
  other arithmetic  47.5 us (16%)
  starting transfers between devices  31.8 us (11%)
  loops' own time  30.2 us (10%)
  waiting for transfers between devices  24 us (8%)
    dot_general x4, matrix products, convolve(): jnp.einsum('kcxy,kcf->fxy', stacked_taps, flat_kernel, preferred_element_...  59.4 us
    while x54, local copies, waits for them, and re-layouts  58.1 us
    another operation x1, loops' own time, on_device(): lax.map(lambda member_pair: slot_canvas(member_pair[0], member_pair[1]),...  30.2 us
    reduce_sum x8, other arithmetic, group_norm(): jnp.mean(jnp.square(grouped - center), axis=(1, 2, 3), keepdims=True)  22.7 us
    ppermute x2, starting transfers between devices, padded_2(): lax.ppermute(lax.slice_in_dim(block, 0, width, axis=dim), axis, backward)  16 us
    ppermute x4, waiting for transfers between devices, shifted(): lax.ppermute(x, axis, [(i, (i + by) % length) for i in range(length)])  15.6 us
    ppermute x4, starting transfers between devices, shifted(): lax.ppermute(x, axis, [(i, (i + by) % length) for i in range(length)])  13.7 us
    another operation x4, local copies, waits for them, and re-layouts, convolve(): jnp.stack([padded[:, across:across + columns, downward:downward + row_cou...  10.5 us
  transfers between devices with their start and end apart: 8, of which 3 were waited for; matrix products, arithmetic and copies ran while one was open for 1% of the time, Pallas kernels for 0%

commit v1 on v0

v1 whole, which is shorter than its diff:
```python
import functools
import math

import jax
import jax.numpy as jnp
import numpy as np
from jax import lax
from jax.experimental import pallas as pl
from jax.experimental.pallas import tpu as pltpu
from jax.sharding import PartitionSpec as P

MESH = pl.DeviceIdType.MESH

sigma_now = 2.0
sigma_next = 1.0
sigma_data = 0.5
input_scale = 1.0 / math.sqrt(sigma_now**2 + sigma_data**2)
skip_scale = sigma_data**2 / (sigma_now**2 + sigma_data**2)
output_scale = sigma_now * sigma_data / math.sqrt(sigma_now**2 + sigma_data**2)
step_factor = (sigma_next - sigma_now) / sigma_now
norm_epsilon = 1e-05

C = 12
F = 128
BW = 64
PW = 128
H = 128
STRIDE = 200
PAIRS = 8
ROWS = PAIRS * H
CELLS = PW * H
f32, bf16 = jnp.float32, jnp.bfloat16


def group_mean(v):
    lane = lax.broadcasted_iota(jnp.int32, v.shape, 1)
    pair = v + pltpu.roll(v, F - 1, 1)
    four = pair + pltpu.roll(pair, F - 2, 1)
    head = jnp.where(lane % 4 == 0, four, 0.0)
    two = head + pltpu.roll(head, 1, 1)
    return 0.25 * (two + pltpu.roll(two, 2, 1))


def norm_affine(shift, total, squares):
    total = jnp.broadcast_to(jnp.sum(total, axis=0, keepdims=True), (8, F))
    squares = jnp.broadcast_to(jnp.sum(squares, axis=0, keepdims=True), (8, F))
    delta = total / CELLS
    mean = shift + delta
    center = group_mean(mean)
    spread = group_mean((squares / CELLS - delta * delta) + jnp.square(mean - center))
    rstd = 1.0 / jnp.sqrt(spread + norm_epsilon)
    return rstd, -center * rstd


def silu_of_twice(u):
    return u + u * jnp.tanh(u)


def kernel(
    owners,
    offset_ref,
    count_ref,
    noisy_ref,
    cond_ref,
    w_in_ref,
    w_mid_ref,
    w_out_ref,
    mod_ref,
    blend_ref,
    out_ref,
    own_x,
    own_k,
    side_x,
    side_k,
    plane_send,
    plane_side,
    term_send,
    term_side,
    planes_mid,
    term_mid,
    source,
    stacked,
    feats,
    hidden,
    rolled,
    terms,
    w1,
    w2,
    w3,
    local_sem,
    send_sem,
    recv_sem,
):
    me, core = lax.axis_index("owner"), lax.axis_index("ens")
    left = lax.rem(me + owners - 1, owners)
    right = lax.rem(me + 1, owners)
    targets = (right, left)

    barrier = pltpu.get_barrier_semaphore()
    for neighbour in (left, right):
        pl.semaphore_signal(barrier, inc=1, device_id=(neighbour, core), device_id_type=MESH)

    local = [
        pltpu.make_async_copy(noisy_ref, own_x, local_sem.at[0]),
        pltpu.make_async_copy(cond_ref, own_k, local_sem.at[1]),
        pltpu.make_async_copy(w_mid_ref, rolled.at[pl.ds(0, 9)], local_sem.at[2]),
    ]
    for copy in local:
        copy.start()

    def remote(kind, side, source_ref, target_ref):
        return pltpu.make_async_remote_copy(
            src_ref=source_ref,
            dst_ref=target_ref,
            send_sem=send_sem.at[kind, side],
            recv_sem=recv_sem.at[kind, side],
            device_id=(targets[side], core),
            device_id_type=MESH,
        )

    def both(kind, make):
        return [remote(kind, side, *make(side)) for side in range(2)]

    send_x = [
        both(m, lambda side: (noisy_ref.at[m], side_x.at[side, m])) for m in range(2)
    ]
    send_k = both(2, lambda side: (cond_ref, side_k.at[side]))
    send_plane = both(3, lambda side: (plane_send.at[side], plane_side.at[side]))
    send_term = [
        both(4 + m, lambda side: (term_send.at[side, m], term_side.at[side, m]))
        for m in range(2)
    ]

    pl.semaphore_wait(barrier, 2)
    for copy in send_x[0] + send_k:
        copy.start()

    offset, count = offset_ref[0], count_ref[0]
    active = [core * 2 + m < count for m in range(2)]

    terms[0, pl.ds(0, BW)] = jnp.zeros((BW, H), f32)
    terms[0, pl.ds(BW, PW)] = blend_ref[...]
    terms[0, pl.ds(BW + PW, BW)] = jnp.zeros((BW, H), f32)
    for block, target in ((0, plane_send.at[1]), (1, planes_mid), (2, plane_send.at[0])):
        plane = terms[0, pl.ds(BW + BW * block - offset, BW)]
        target[0] = plane
        for m in range(2):
            target[1 + m] = jnp.where(active[m], plane, 0.0)
    for copy in send_plane:
        copy.start()
    terms[:, pl.ds(0, BW)] = jnp.zeros((C, BW, H), f32)
    terms[:, pl.ds(BW + PW, BW)] = jnp.zeros((C, BW, H), f32)

    taps = w_in_ref[...].astype(f32)
    zeros8, zeros32 = jnp.zeros((8, F), f32), jnp.zeros((32, F), f32)
    zeros128 = jnp.zeros((F, F), bf16)
    for ci in range(4):
        for p in range(2):
            a = ci - p
            if 0 <= a < 3:
                pieces = []
                for b in range(3):
                    pieces += [taps[(a * 3 + b) * 24 : (a * 3 + b) * 24 + 24], zeros8]
                block = jnp.concatenate(pieces + [zeros32], axis=0).astype(bf16)
            else:
                block = zeros128
            w1[pl.ds(ci * 128, 128), pl.ds(p * 128, 128)] = block
    out_rows = jnp.concatenate([w_out_ref[...].astype(f32), jnp.zeros((4, F), f32)], axis=0)
    spread_rows = jnp.broadcast_to(out_rows[:, None, :], (16, 8, F)).reshape(F, F).T
    lane = lax.broadcasted_iota(jnp.int32, (F, F), 1)
    for k in range(8):
        w3[pl.ds(k * 128, 128)] = jnp.where(lane % 8 == k, spread_rows, 0.0).astype(bf16)
    local[2].wait()
    for b in range(3):
        for ci in range(4):
            for p in range(2):
                a = ci - p
                block = rolled[a * 3 + b] if 0 <= a < 3 else zeros128
                w2[pl.ds((b * 4 + ci) * 128, 128), pl.ds(p * 128, 128)] = block

    for ref in (stacked,):
        ref[0, 0] = zeros128
        ref[1, BW] = zeros128
    for b in range(3):
        hidden[b, 0, 0] = zeros128
        hidden[b, 1, BW] = zeros128

    def put_state(ref, block):
        for c in range(C):
            scaled = (input_scale * ref[c].astype(f32)).astype(bf16).astype(f32)
            source[pl.ds(c * STRIDE + block * BW, BW)] = scaled

    def put_cond(ref, block):
        for c in range(C):
            source[pl.ds((C + c) * STRIDE + block * BW, BW)] = ref[c].astype(f32)

    local[0].wait()
    local[1].wait()
    put_cond(own_k, 1)
    for copy in send_k:
        copy.wait_recv()
    put_cond(side_k.at[0], 0)
    put_cond(side_k.at[1], 2)

    def stack_column(column):
        v = source[pl.ds(offset + column, 24, stride=STRIDE), :]
        row = lax.broadcasted_iota(jnp.int32, v.shape, 1)
        before = jnp.where(row == 0, 0.0, pltpu.roll(v, 1, 1))
        after = jnp.where(row == H - 1, 0.0, pltpu.roll(v, H - 1, 1))
        full = jnp.concatenate([before, zeros8, v, zeros8, after, zeros8, zeros32], axis=0)
        return full.T.astype(bf16)

    def stack_step(i, carry):
        for s in range(8):
            slot = i * 8 + s
            stacked[1, slot] = stack_column(2 * slot)
            stacked[0, slot + 1] = stack_column(2 * slot + 1)
        return carry

    def gather(refs, step):
        columns = []
        for ref in refs:
            for ci in range(4):
                part = ref[ci % 2, pl.ds(step * PAIRS + ci // 2, PAIRS)]
                columns.append(part.reshape(ROWS, F))
        return jnp.concatenate(columns, axis=1)

    def conv_step(step, carry, refs, w, add):
        shift, total, squares = carry
        acc = jnp.dot(gather(refs, step), w[...], preferred_element_type=f32)
        halves = []
        for p in range(2):
            half = acc[:, p * F : (p + 1) * F].reshape(PAIRS, H, F)
            if add:
                half = half + feats[p, pl.ds(step * PAIRS, PAIRS)]
            feats[p, pl.ds(step * PAIRS, PAIRS)] = half
            halves.append(half.reshape(ROWS // 8, 8, F))
        if shift is None:
            shift = (jnp.sum(halves[0], axis=0) + jnp.sum(halves[1], axis=0)) / (2 * ROWS // 8)
            shift = jnp.broadcast_to(jnp.mean(shift, axis=0, keepdims=True), (8, F))
        for half in halves:
            deviation = half - shift
            total = total + jnp.sum(deviation, axis=0)
            squares = squares + jnp.sum(deviation * deviation, axis=0)
        return shift, total, squares

    def conv(refs, w, add):
        zero = jnp.zeros((8, F), f32)
        carry = conv_step(0, (None, zero, zero), refs, w, add)
        step = functools.partial(conv_step, refs=refs, w=w, add=add)
        return lax.fori_loop(1, BW // PAIRS, step, carry)

    def hidden_step(i, carry):
        scale, bias = carry
        for s in range(4):
            slot = i * 4 + s
            for p in range(2):
                h = silu_of_twice(feats[p, slot] * scale + bias)
                row = lax.broadcasted_iota(jnp.int32, h.shape, 0)
                before = jnp.where(row == 0, 0.0, pltpu.roll(h, 1, 0))
                after = jnp.where(row == H - 1, 0.0, pltpu.roll(h, H - 1, 0))
                for b, value in enumerate((before, h, after)):
                    hidden[b, 1 - p, slot + p] = value.astype(bf16)
        return carry

    def out_step(i, carry):
        scale, bias = carry
        columns = []
        for k in range(8):
            rows = []
            for g in range(4):
                u = feats[k % 2, i * 16 + g * 4 + k // 2] * scale + bias
                rows.append(silu_of_twice(u).astype(bf16))
            columns.append(jnp.concatenate(rows, axis=0))
        result = jnp.dot(
            jnp.concatenate(columns, axis=1), w3[...], preferred_element_type=f32
        )
        for g in range(4):
            flipped = result[g * H : (g + 1) * H].T.reshape(16, 8, H)[:C]
            weight = blend_ref[pl.ds(i * 32 + g * 8, 8)] * (-step_factor * output_scale)
            terms[:, pl.ds(BW + i * 32 + g * 8, 8)] = flipped * weight
        return carry

    for m in range(2):
        put_state(own_x.at[m], 1)
        for copy in send_x[m]:
            copy.wait_recv()
        if m == 0:
            for copy in send_x[1]:
                copy.start()
        put_state(side_x.at[0, m], 0)
        put_state(side_x.at[1, m], 2)
        lax.fori_loop(0, 8, stack_step, 0)
        scale, bias = norm_affine(*conv((stacked,), w1, False))
        gain = 1.0 + mod_ref[0:1]
        scale, bias = scale * gain * 0.5, (bias * gain + mod_ref[1:2]) * 0.5
        lax.fori_loop(0, 16, hidden_step, (scale[0:1], bias[0:1]))
        scale, bias = norm_affine(*conv([hidden.at[b] for b in range(3)], w2, True))
        lax.fori_loop(0, 4, out_step, (scale[0:1] * 0.5, bias[0:1] * 0.5))
        for block, target in (
            (0, term_send.at[1, m]),
            (2, term_send.at[0, m]),
            (1, term_mid.at[m]),
        ):
            for c in range(C):
                part = terms[c, pl.ds(BW + BW * block - offset, BW)]
                target[c] = jnp.where(active[m], part, 0.0)
            if block == 2:
                for copy in send_term[m]:
                    copy.start()

    for copy in send_plane:
        copy.wait_recv()
    planes = [planes_mid[q] + plane_side[0, q] + plane_side[1, q] for q in range(3)]
    inverse = 1.0 / planes[0]
    for m in range(2):
        for copy in send_term[m]:
            copy.wait_recv()
        factor = planes[1 + m] * (step_factor * (1.0 - skip_scale))
        for c in range(C):
            x = own_x[m, c].astype(f32)
            numerator = term_mid[m, c] + term_side[0, m, c] + term_side[1, m, c]
            out_ref[m, c] = x + (x * factor + numerator) * inverse

    for copy in send_x[0] + send_x[1] + send_k + send_plane + send_term[0] + send_term[1]:
        copy.wait_send()


def solution(mesh):
    owners = mesh.shape["owner"]
    places = (np.arange(PW) + 0.5).astype(np.float32)
    blend = 0.1 + np.sin(np.float32(math.pi) * places / np.float32(PW)) ** 2
    blend = np.broadcast_to(blend.astype(np.float32)[:, None], (PW, H))

    def on_device(noisy, cond, counts, offsets, w_in, w_mid, w_out, mod):
        smem = pl.BlockSpec(memory_space=pltpu.SMEM)
        vmem = pl.BlockSpec(memory_space=pltpu.VMEM)
        hbm = pl.BlockSpec(memory_space=pl.ANY)
        return pl.pallas_call(
            functools.partial(kernel, owners),
            out_shape=jax.ShapeDtypeStruct((2, C, BW, H), f32),
            in_specs=[smem, smem, hbm, hbm, vmem, hbm, vmem, vmem, vmem],
            out_specs=vmem,
            scratch_shapes=[
                pltpu.VMEM((2, C, BW, H), bf16),
                pltpu.VMEM((C, BW, H), bf16),
                pltpu.VMEM((2, 2, C, BW, H), bf16),
                pltpu.VMEM((2, C, BW, H), bf16),
                pltpu.VMEM((2, 3, BW, H), f32),
                pltpu.VMEM((2, 3, BW, H), f32),
                pltpu.VMEM((2, 2, C, BW, H), f32),
                pltpu.VMEM((2, 2, C, BW, H), f32),
                pltpu.VMEM((3, BW, H), f32),
                pltpu.VMEM((2, C, BW, H), f32),
                pltpu.VMEM((2 * C * STRIDE, H), f32),
                pltpu.VMEM((2, BW + 1, H, F), bf16),
                pltpu.VMEM((2, BW, H, F), f32),
                pltpu.VMEM((3, 2, BW + 1, H, F), bf16),
                pltpu.VMEM((9, F, F), bf16),
                pltpu.VMEM((C, 2 * PW, H), f32),
                pltpu.VMEM((4 * F, 2 * F), bf16),
                pltpu.VMEM((12 * F, 2 * F), bf16),
                pltpu.VMEM((8 * F, F), bf16),
                pltpu.SemaphoreType.DMA((3,)),
                pltpu.SemaphoreType.DMA((6, 2)),
                pltpu.SemaphoreType.DMA((6, 2)),
            ],
            compiler_params=pltpu.CompilerParams(
                collective_id=0, has_side_effects=True, vmem_limit_bytes=56 * 2**20
            ),
            cost_estimate=pl.CostEstimate(
                flops=24 * 10**9, bytes_accessed=4 * 10**6, transcendentals=8 * 10**6
            ),
        )(
            offsets,
            counts,
            noisy,
            cond,
            w_in.reshape(216, F),
            w_mid.reshape(9, F, F),
            w_out,
            mod,
            jnp.asarray(blend),
        )

    placed = (
        P("ens", None, "owner", None),
        P(None, "owner", None),
        P("owner"),
        P("owner"),
        P(),
        P(),
        P(),
        P(),
    )
    return jax.shard_map(
        on_device,
        mesh=mesh,
        in_specs=placed,
        out_specs=P("ens", None, "owner", None),
        check_vma=False,
    )
```

time: 288 us -> 85.6 us (0.30); the launches traced: 282 us -> 85.3 us
  Pallas kernels: 0 us -> 80.5 us
  local copies, waits for them, and re-layouts: 78.9 us -> 3.45 us
  matrix products: 69 us -> 0 us
  other arithmetic: 47.5 us -> 0 us
  starting transfers between devices: 31.8 us -> 0 us
  loops' own time: 30.2 us -> 0 us
  waiting for transfers between devices: 24 us -> 0 us
    pallas_call x0 -> x1, Pallas kernels: none -> 80.5 us  [on_device(): pl.pallas_call(functools.partial(kernel, owners), out_shape=jax.ShapeDtyp...]
    dot_general x6 -> x0, matrix products: 69 us -> none  [the longest x4 59.4 us: convolve(): jnp.einsum('kcxy,kcf->fxy', stacked_taps, flat_kernel, preferred_element_...]
    while x54 -> x0, local copies, waits for them, and re-layouts: 58.1 us -> none
    ppermute x8 -> x0, starting transfers between devices: 31.8 us -> none  [the longest x2 16 us: padded_2(): lax.ppermute(lax.slice_in_dim(block, 0, width, axis=dim), axis, backward)]
    another operation x1 -> x0, loops' own time: 30.2 us -> none  [on_device(): lax.map(lambda member_pair: slot_canvas(member_pair[0], member_pair[1]),...]
    ppermute x8 -> x0, waiting for transfers between devices: 24 us -> none  [the longest x4 15.6 us: shifted(): lax.ppermute(x, axis, [(i, (i + by) % length) for i in range(length)])]
    reduce_sum x12 -> x0, other arithmetic: 23.1 us -> none  [the longest x8 22.7 us: group_norm(): jnp.mean(jnp.square(grouped - center), axis=(1, 2, 3), keepdims=True)]
    convert_element_type x4 -> x0, other arithmetic: 10.2 us -> none  [the longest x2 9.93 us: member_update(): hidden = jax.nn.silu(modulated).astype(jnp.bfloat16)]
  transfers between devices with their start and end apart: 8 -> 0, of which waited for: 3 -> 0; matrix products, arithmetic and copies ran while one was open for 1% -> 0% of each run, Pallas kernels for 0% -> 0%
where the time goes in v1:
time: 85.6 us; the launch traced here: 85.3 us
  Pallas kernels  80.5 us (94%)
  local copies, waits for them, and re-layouts  3.45 us (4%)
  between operations  1.31 us (2%)
    pallas_call x1, Pallas kernels, on_device(): pl.pallas_call(functools.partial(kernel, owners), out_shape=jax.ShapeDtyp...  80.5 us
    unnamed x3, local copies, waits for them, and re-layouts  2.74 us

profile of v1, /device:TPU:1, one launch (start us, length us, event | category | flops | bytes accessed | tf_op | source)
XLA Modules:
  0.0 85.3 jit_solution(643239644882093947)
XLA Ops:
  1.3 0.0 copy-start
  1.3 0.6 copy-done
  2.0 0.7 jit_solution_.3.blend_ref
  2.7 80.5 %shard_map.91 = f32[2,12,64,128]{3,2,1,0:T(8,128)} custom-call(s32[1]{0:T(128)S(6)} %copy.12.offset_ref, s32[1]{0:T(128)S(6)} %copy.11.count_ref, bf16[2,12,64,128]{3,2,1,0:T(8,128)(2,1)} %noisy_ref.1, bf16[12,64,128]{2,1,0:T(8,128)(2,1)} %cond_ref.1, bf16[216,128]{1,0:T(8,128)(2,1)} %bitcast.3, bf16[9,128,128]{2,1,0:T(8,128)(2,1)} %bitcast.2, ...), custom_call_target="tpu_custom_call" | custom-call | flops 24000000000 | bytes 4000000 | tf_op jit(solution)/shard_map/pallas_call | solution.py:339
  83.2 2.1 %copy.13 = f32[2,12,64,128]{3,2,1,0:T(8,128)} copy(f32[2,12,64,128]{3,2,1,0:T(8,128)} %shard_map.91) | data formatting | bytes 1572864
Async XLA Ops:
  1.3 0.7 copy-start

commit v2 on v1

v2 whole, which is shorter than its diff:
```python
import functools
import math

import jax
import jax.numpy as jnp
import numpy as np
from jax import lax
from jax.experimental import pallas as pl
from jax.experimental.pallas import tpu as pltpu
from jax.sharding import PartitionSpec as P

MESH = pl.DeviceIdType.MESH

sigma_now = 2.0
sigma_next = 1.0
sigma_data = 0.5
input_scale = 1.0 / math.sqrt(sigma_now**2 + sigma_data**2)
skip_scale = sigma_data**2 / (sigma_now**2 + sigma_data**2)
output_scale = sigma_now * sigma_data / math.sqrt(sigma_now**2 + sigma_data**2)
step_factor = (sigma_next - sigma_now) / sigma_now
norm_epsilon = 1e-05

C = 12
F = 128
BW = 64
PW = 128
H = 128
STRIDE = 200
LANES = 40
PAIRS = 8
OWN = 30
OWN_STEP = 10
REST_STEP = 12
CELLS = PW * H
LEVELS = 32767.0
f32, bf16 = jnp.float32, jnp.bfloat16


def group_mean(v):
    lane = lax.broadcasted_iota(jnp.int32, v.shape, 1)
    pair = v + pltpu.roll(v, F - 1, 1)
    four = pair + pltpu.roll(pair, F - 2, 1)
    head = jnp.where(lane % 4 == 0, four, 0.0)
    two = head + pltpu.roll(head, 1, 1)
    return 0.25 * (two + pltpu.roll(two, 2, 1))


def merge(stats, count, total, squares):
    number, mean, spread = stats
    total = jnp.broadcast_to(jnp.sum(total, axis=0, keepdims=True), (8, F))
    squares = jnp.broadcast_to(jnp.sum(squares, axis=0, keepdims=True), (8, F))
    number = number + count
    return number, mean + total / number, spread + (squares - total * total / number)


def norm_affine(mean, squares):
    center = group_mean(mean)
    spread = group_mean(squares / CELLS + jnp.square(mean - center))
    rstd = 1.0 / jnp.sqrt(spread + norm_epsilon)
    return rstd, -center * rstd


def silu_of_twice(u):
    return u + u * jnp.tanh(u)


def kernel(
    owners,
    offset_ref,
    count_ref,
    noisy_ref,
    cond_ref,
    w_in_ref,
    w_mid_ref,
    w_out_ref,
    mod_ref,
    blend_ref,
    out_ref,
    own_x,
    own_k,
    side_x,
    side_k,
    plane_send,
    plane_side,
    term_send,
    term_side,
    step_send,
    step_side,
    planes_mid,
    term_mid,
    source,
    stacked,
    ring1,
    ring1b,
    feats,
    sums,
    ring2,
    ring2b,
    rolled,
    terms,
    w1,
    w1b,
    w2,
    w3,
    local_sem,
    send_sem,
    recv_sem,
):
    me, core = lax.axis_index("owner"), lax.axis_index("ens")
    left = lax.rem(me + owners - 1, owners)
    right = lax.rem(me + 1, owners)
    targets = (right, left)

    barrier = pltpu.get_barrier_semaphore()
    for neighbour in (left, right):
        pl.semaphore_signal(barrier, inc=1, device_id=(neighbour, core), device_id_type=MESH)

    local = [
        pltpu.make_async_copy(noisy_ref, own_x, local_sem.at[0]),
        pltpu.make_async_copy(cond_ref, own_k, local_sem.at[1]),
        pltpu.make_async_copy(w_mid_ref, rolled, local_sem.at[2]),
    ]
    for copy in local:
        copy.start()

    def both(kind, make):
        copies = []
        for side in range(2):
            source_ref, target_ref = make(side)
            copies.append(
                pltpu.make_async_remote_copy(
                    src_ref=source_ref,
                    dst_ref=target_ref,
                    send_sem=send_sem.at[kind, side],
                    recv_sem=recv_sem.at[kind, side],
                    device_id=(targets[side], core),
                    device_id_type=MESH,
                )
            )
        return copies

    send_x = [
        both(m, lambda side: (noisy_ref.at[m], side_x.at[side, m])) for m in range(2)
    ]
    send_k = both(2, lambda side: (cond_ref, side_k.at[side]))
    send_plane = both(3, lambda side: (plane_send.at[side], plane_side.at[side]))
    send_term = [
        both(4 + m, lambda side: (term_send.at[side, m], term_side.at[side, m]))
        for m in range(2)
    ]
    send_step = [
        both(6 + m, lambda side: (step_send.at[side, m], step_side.at[side, m]))
        for m in range(2)
    ]

    pl.semaphore_wait(barrier, 2)
    for copy in send_x[0] + send_k:
        copy.start()

    offset, count = offset_ref[0], count_ref[0]
    active = [core * 2 + m < count for m in range(2)]
    odd = offset & 1
    even = offset - odd
    left_pairs = 33 - (offset >> 1)

    taps = w_in_ref[...].astype(f32)
    zeros128 = jnp.zeros((F, F), bf16)
    zeros8, zeros16 = jnp.zeros((8, F), f32), jnp.zeros((16, F), f32)
    for ci in range(4):
        for p in range(2):
            a = ci - p
            block = block_b = zeros128
            if 0 <= a < 3:
                pieces, pieces_b = [], []
                for b in range(3):
                    tap = taps[(a * 3 + b) * 24 : (a * 3 + b) * 24 + 24]
                    pieces += [tap, zeros16]
                    pieces_b += [zeros16[:C], tap[C:], tap[:C], zeros16[:4]]
                block = jnp.concatenate(pieces + [zeros8], axis=0).astype(bf16)
                block_b = jnp.concatenate(pieces_b + [zeros8], axis=0).astype(bf16)
            w1[pl.ds(ci * 128, 128), pl.ds(p * 128, 128)] = block
            w1b[pl.ds(ci * 128, 128), pl.ds(p * 128, 128)] = block_b

    def put_state(ref, slot, block):
        for c in range(C):
            scaled = (input_scale * ref[c].astype(f32)).astype(bf16).astype(f32)
            source[pl.ds((slot + c) * STRIDE + block * BW, BW)] = scaled

    def put_cond(ref, block):
        for c in range(C):
            source[pl.ds((C + c) * STRIDE + block * BW, BW)] = ref[c].astype(f32)

    local[0].wait()
    local[1].wait()
    source[pl.ds(36 * STRIDE, 4 * STRIDE)] = jnp.zeros((4 * STRIDE, H), f32)
    put_cond(own_k, 1)
    put_state(own_x.at[0], 0, 1)
    put_state(own_x.at[1], 24, 1)

    def stack_column(column, channels, valid=None):
        v = source[pl.ds(column, channels, stride=STRIDE), :]
        if valid is not None:
            v = jnp.where(valid, v, 0.0)
        row = lax.broadcasted_iota(jnp.int32, v.shape, 1)
        before = jnp.where(row == 0, 0.0, pltpu.roll(v, 1, 1))
        after = jnp.where(row == H - 1, 0.0, pltpu.roll(v, H - 1, 1))
        pieces = []
        for part in (before, v, after):
            pieces += [part] if channels == LANES else [part, zeros16]
        return jnp.concatenate(pieces + [zeros8], axis=0).T.astype(bf16)

    def own_stack_step(i, carry):
        for t in range(16):
            stacked[t % 2, i * 8 + t // 2] = stack_column(BW + 1 + i * 16 + t, LANES)
        return carry

    lax.fori_loop(0, 4, own_stack_step, 0)

    def deviations(stats, values, keep=None):
        deviation = values.reshape(-1, 8, F) - stats[1]
        if keep is not None:
            deviation = jnp.where(keep, deviation, 0.0)
        return jnp.sum(deviation, axis=0), jnp.sum(deviation * deviation, axis=0)

    def own_conv(m):
        def step(i, stats):
            columns = []
            for ci in range(4):
                part = stacked[ci % 2, pl.ds(i * OWN_STEP + ci // 2, OWN_STEP)]
                columns.append(part.reshape(OWN_STEP * H, F))
            lhs = jnp.concatenate(columns, axis=1)
            acc = jnp.dot(lhs, (w1, w1b)[m][...], preferred_element_type=f32)
            total = squares = jnp.zeros((8, F), f32)
            for p in range(2):
                half = acc[:, p * F : (p + 1) * F]
                feats[p, pl.ds(m * OWN + i * OWN_STEP, OWN_STEP)] = half.reshape(
                    OWN_STEP, H, F
                )
                more = deviations(stats, half)
                total, squares = total + more[0], squares + more[1]
            return merge(stats, 2.0 * OWN_STEP * H, total, squares)

        zero = jnp.zeros((8, F), f32)
        return lax.fori_loop(0, OWN // OWN_STEP, step, (zero, zero, zero))

    own_stats = [own_conv(m) for m in range(2)]

    terms[0, pl.ds(0, BW)] = jnp.zeros((BW, H), f32)
    terms[0, pl.ds(BW, PW)] = blend_ref[...]
    terms[0, pl.ds(BW + PW, BW)] = jnp.zeros((BW, H), f32)
    for block, target in ((0, plane_send.at[1]), (1, planes_mid), (2, plane_send.at[0])):
        plane = terms[0, pl.ds(BW + BW * block - offset, BW)]
        target[0] = plane
        for m in range(2):
            target[1 + m] = jnp.where(active[m], plane, 0.0)
    for copy in send_plane:
        copy.start()
    terms[:, pl.ds(0, BW)] = jnp.zeros((C, BW, H), f32)
    terms[:, pl.ds(BW + PW, BW)] = jnp.zeros((C, BW, H), f32)

    out_rows = jnp.concatenate([w_out_ref[...].astype(f32), jnp.zeros((4, F), f32)], axis=0)
    spread_rows = jnp.broadcast_to(out_rows[:, None, :], (16, 8, F)).reshape(F, F).T
    lane = lax.broadcasted_iota(jnp.int32, (F, F), 1)
    for k in range(8):
        w3[pl.ds(k * 128, 128)] = jnp.where(lane % 8 == k, spread_rows, 0.0).astype(bf16)
    local[2].wait()
    for b in range(3):
        for ci in range(4):
            for p in range(2):
                a = ci - p
                block = rolled[a * 3 + b] if 0 <= a < 3 else zeros128
                w2[pl.ds((b * 4 + ci) * 128, 128), pl.ds(p * 128, 128)] = block

    rings1, rings2 = (ring1, ring1b), (ring2, ring2b)

    def rest_stack(g):
        for t in range(2 * REST_STEP + 4):
            place = 2 * REST_STEP * g + t
            first_right = 68 - even
            column = jnp.where(place < first_right, even - 1 + place, 125 - first_right + place)
            valid = (column >= offset) & (column < offset + PW)
            column = jnp.clip(column, 0, STRIDE - 1)
            rings1[g % 2][t % 2, t // 2] = stack_column(column, 24, valid)

    def rest_conv(g, m, stats):
        columns = []
        for ci in range(4):
            parts = []
            for p in range(REST_STEP):
                skip = (REST_STEP * g + p >= left_pairs).astype(jnp.int32)
                parts.append(rings1[g % 2][ci % 2, p + ci // 2 + skip])
            columns.append(jnp.concatenate(parts, axis=0))
        lhs = jnp.concatenate(columns, axis=1)
        acc = jnp.dot(lhs, w1[...], preferred_element_type=f32)
        total = squares = jnp.zeros((8, F), f32)
        number = 2.0 * REST_STEP * H
        for p in range(2):
            half = acc[:, p * F : (p + 1) * F]
            feats[p, pl.ds(2 * OWN + g * REST_STEP, REST_STEP)] = half.reshape(REST_STEP, H, F)
            start, stop = 0, REST_STEP * H
            if g == 0 and p == 0:
                start = H
                more = deviations(stats, half[:H], odd == 0)
                total, squares = total + more[0], squares + more[1]
                number = number - odd.astype(f32) * H
            if g == 2:
                stop = (REST_STEP - 2) * H
                if p == 0:
                    more = deviations(stats, half[stop : stop + H], odd == 1)
                    total, squares = total + more[0], squares + more[1]
                    number = number - 4.0 * H + odd.astype(f32) * H
            more = deviations(stats, half[start:stop])
            total, squares = total + more[0], squares + more[1]
        return merge(stats, number, total, squares)

    def first_at(m, column):
        place = offset + column
        pair, parity = place >> 1, place & 1
        rest = 2 * OWN + jnp.where(pair < 33, pair - (offset >> 1), pair - 63 + left_pairs)
        own = m * OWN + pair - 33
        slot = jnp.where((pair >= 33) & (pair < 63), own, rest)
        return feats[parity, slot]

    def put_hidden(m, affine, column, places):
        h = silu_of_twice(first_at(m, jnp.minimum(column, PW - 1)) * affine[0] + affine[1])
        if any(t == 2 * PAIRS + 1 for _, t in places):
            h = jnp.where(column < PW, h, 0.0)
        row = lax.broadcasted_iota(jnp.int32, h.shape, 0)
        before = jnp.where(row == 0, 0.0, pltpu.roll(h, 1, 0))
        after = jnp.where(row == H - 1, 0.0, pltpu.roll(h, H - 1, 0))
        for b, value in enumerate((before, h, after)):
            for ref, t in places:
                ref[b, t % 2, t // 2] = value.astype(bf16)

    def fill(m, affine, g, here, there):
        for r in range(2 * PAIRS):
            places = [(here, r + 2)]
            if r >= 2 * PAIRS - 2:
                places.append((there, r + 2 - 2 * PAIRS))
            put_hidden(m, affine, 2 * PAIRS * g + 1 + r, places)

    def mid_conv(m, g, ref, stats):
        columns = []
        for b in range(3):
            for ci in range(4):
                part = ref[b, ci % 2, pl.ds(ci // 2, PAIRS)]
                columns.append(part.reshape(PAIRS * H, F))
        acc = jnp.dot(jnp.concatenate(columns, axis=1), w2[...], preferred_element_type=f32)
        total = squares = jnp.zeros((8, F), f32)
        for q in range(PAIRS):
            for p in range(2):
                both_convs = acc[q * H : (q + 1) * H, p * F : (p + 1) * F]
                both_convs = both_convs + first_at(m, 2 * (PAIRS * g + q) + p)
                sums[p, PAIRS * g + q] = both_convs
                more = deviations(stats, both_convs)
                total, squares = total + more[0], squares + more[1]
        return merge(stats, 2.0 * PAIRS * H, total, squares)

    def mid_step(i, carry, m):
        stats, affine = carry
        stats = mid_conv(m, 2 * i, ring2, stats)
        fill(m, affine, 2 * i + 1, ring2b, ring2)
        stats = mid_conv(m, 2 * i + 1, ring2b, stats)
        fill(m, affine, 2 * i + 2, ring2, ring2b)
        return stats, affine

    def out_step(i, carry):
        scale, bias = carry
        for sub in range(2):
            base = i * 32 + sub * 16
            columns = []
            for k in range(8):
                rows = []
                for g in range(4):
                    u = sums[k % 2, base + g * 4 + k // 2] * scale + bias
                    rows.append(silu_of_twice(u).astype(bf16))
                columns.append(jnp.concatenate(rows, axis=0))
            result = jnp.dot(
                jnp.concatenate(columns, axis=1), w3[...], preferred_element_type=f32
            )
            for g in range(4):
                flipped = result[g * H : (g + 1) * H].T.reshape(16, 8, H)[:C]
                at = 2 * base + g * 8
                weight = blend_ref[pl.ds(at, 8)] * (-step_factor * output_scale)
                terms[:, pl.ds(BW + at, 8)] = flipped * weight
        return carry

    for copy in send_k:
        copy.wait_recv()
    put_cond(side_k.at[0], 0)
    put_cond(side_k.at[1], 2)

    for m in range(2):
        if m == 1:
            put_state(own_x.at[m], 0, 1)
        for copy in send_x[m]:
            copy.wait_recv()
        if m == 0:
            for copy in send_x[1]:
                copy.start()
        put_state(side_x.at[0, m], 0, 0)
        put_state(side_x.at[1, m], 0, 2)
        stats = own_stats[m]
        rest_stack(0)
        for g in range(3):
            if g < 2:
                rest_stack(g + 1)
            stats = rest_conv(g, m, stats)
        scale, bias = norm_affine(stats[1], stats[2])
        gain = 1.0 + mod_ref[0:1]
        scale, bias = scale * gain * 0.5, (bias * gain + mod_ref[1:2]) * 0.5
        affine = scale[0:1], bias[0:1]
        for b in range(3):
            ring2[b, 0, 0] = zeros128
        put_hidden(m, affine, jnp.int32(0), [(ring2, 1)])
        fill(m, affine, 0, ring2, ring2b)
        zero = jnp.zeros((8, F), f32)
        (stats, _) = lax.fori_loop(
            0,
            BW // PAIRS // 2,
            functools.partial(mid_step, m=m),
            ((zero, stats[1], zero), affine),
        )
        scale, bias = norm_affine(stats[1], stats[2])
        lax.fori_loop(0, 2, out_step, (scale[0:1] * 0.5, bias[0:1] * 0.5))
        for block, side in ((0, 1), (2, 0)):
            largest = jnp.full((8, H), 1e-30, f32)
            for c in range(C):
                part = terms[c, pl.ds(BW + BW * block - offset, BW)]
                part = jnp.max(jnp.abs(part).reshape(8, 8, H), axis=0)
                largest = jnp.maximum(largest, part)
            step_send[side, m] = jnp.where(active[m], largest * (1.0 / LEVELS), 0.0)
            inverse = LEVELS / largest
            for c in range(C):
                part = terms[c, pl.ds(BW + BW * block - offset, BW)].reshape(8, 8, H)
                levels = jnp.round(part * inverse).astype(jnp.int32)
                term_send[side, m, c] = levels.reshape(BW, H).astype(jnp.int16)
            send_term[m][side].start()
            send_step[m][side].start()
        for c in range(C):
            part = terms[c, pl.ds(2 * BW - offset, BW)]
            term_mid[m, c] = jnp.where(active[m], part, 0.0)

    for copy in send_plane:
        copy.wait_recv()
    planes = [planes_mid[q] + plane_side[0, q] + plane_side[1, q] for q in range(3)]
    inverse = 1.0 / planes[0]
    for m in range(2):
        for copy in send_step[m] + send_term[m]:
            copy.wait_recv()
        factor = planes[1 + m] * (step_factor * (1.0 - skip_scale))
        steps = [step_side[side, m] for side in range(2)]
        for c in range(C):
            x = own_x[m, c].astype(f32)
            numerator = term_mid[m, c]
            for side in range(2):
                levels = term_side[side, m, c].astype(jnp.int32).astype(f32)
                numerator = numerator + (levels.reshape(8, 8, H) * steps[side]).reshape(BW, H)
            out_ref[m, c] = x + (x * factor + numerator) * inverse

    sent = send_k + send_plane
    for m in range(2):
        sent = sent + send_x[m] + send_term[m] + send_step[m]
    for copy in sent:
        copy.wait_send()


def solution(mesh):
    owners = mesh.shape["owner"]
    places = (np.arange(PW) + 0.5).astype(np.float32)
    blend = 0.1 + np.sin(np.float32(math.pi) * places / np.float32(PW)) ** 2
    blend = np.broadcast_to(blend.astype(np.float32)[:, None], (PW, H))

    def on_device(noisy, cond, counts, offsets, w_in, w_mid, w_out, mod):
        smem = pl.BlockSpec(memory_space=pltpu.SMEM)
        vmem = pl.BlockSpec(memory_space=pltpu.VMEM)
        hbm = pl.BlockSpec(memory_space=pl.ANY)
        return pl.pallas_call(
            functools.partial(kernel, owners),
            out_shape=jax.ShapeDtypeStruct((2, C, BW, H), f32),
            in_specs=[smem, smem, hbm, hbm, vmem, hbm, vmem, vmem, vmem],
            out_specs=vmem,
            scratch_shapes=[
                pltpu.VMEM((2, C, BW, H), bf16),
                pltpu.VMEM((C, BW, H), bf16),
                pltpu.VMEM((2, 2, C, BW, H), bf16),
                pltpu.VMEM((2, C, BW, H), bf16),
                pltpu.VMEM((2, 3, BW, H), f32),
                pltpu.VMEM((2, 3, BW, H), f32),
                pltpu.VMEM((2, 2, C, BW, H), jnp.int16),
                pltpu.VMEM((2, 2, C, BW, H), jnp.int16),
                pltpu.VMEM((2, 2, 8, H), f32),
                pltpu.VMEM((2, 2, 8, H), f32),
                pltpu.VMEM((3, BW, H), f32),
                pltpu.VMEM((2, C, BW, H), f32),
                pltpu.VMEM((LANES * STRIDE, H), f32),
                pltpu.VMEM((2, BW // 2, H, F), bf16),
                pltpu.VMEM((2, REST_STEP + 2, H, F), bf16),
                pltpu.VMEM((2, REST_STEP + 2, H, F), bf16),
                pltpu.VMEM((2, 2 * OWN + 3 * REST_STEP, H, F), f32),
                pltpu.VMEM((2, BW, H, F), f32),
                pltpu.VMEM((3, 2, PAIRS + 1, H, F), bf16),
                pltpu.VMEM((3, 2, PAIRS + 1, H, F), bf16),
                pltpu.VMEM((9, F, F), bf16),
                pltpu.VMEM((C, 2 * PW, H), f32),
                pltpu.VMEM((4 * F, 2 * F), bf16),
                pltpu.VMEM((4 * F, 2 * F), bf16),
                pltpu.VMEM((12 * F, 2 * F), bf16),
                pltpu.VMEM((8 * F, F), bf16),
                pltpu.SemaphoreType.DMA((3,)),
                pltpu.SemaphoreType.DMA((8, 2)),
                pltpu.SemaphoreType.DMA((8, 2)),
            ],
            compiler_params=pltpu.CompilerParams(
                collective_id=0, has_side_effects=True, vmem_limit_bytes=56 * 2**20
            ),
            cost_estimate=pl.CostEstimate(
                flops=24 * 10**9, bytes_accessed=4 * 10**6, transcendentals=8 * 10**6
            ),
        )(
            offsets,
            counts,
            noisy,
            cond,
            w_in.reshape(216, F),
            w_mid.reshape(9, F, F),
            w_out,
            mod,
            jnp.asarray(blend),
        )

    placed = (
        P("ens", None, "owner", None),
        P(None, "owner", None),
        P("owner"),
        P("owner"),
        P(),
        P(),
        P(),
        P(),
    )
    return jax.shard_map(
        on_device,
        mesh=mesh,
        in_specs=placed,
        out_specs=P("ens", None, "owner", None),
        check_vma=False,
    )
```

time: 85.6 us -> 67.9 us (0.79)
  Pallas kernels: 80.5 us -> 62.6 us
    pallas_call x1, Pallas kernels: 80.5 us -> 62.6 us  [on_device(): pl.pallas_call(functools.partial(kernel, owners), out_shape=jax.ShapeDtyp...]
where the time goes in v2:
time: 67.9 us; the launch traced here: 67.4 us
  Pallas kernels  62.6 us (92%)
  local copies, waits for them, and re-layouts  3.45 us (5%)
  between operations  1.32 us (2%)
    pallas_call x1, Pallas kernels, on_device(): pl.pallas_call(functools.partial(kernel, owners), out_shape=jax.ShapeDtyp...  62.6 us
    unnamed x3, local copies, waits for them, and re-layouts  2.74 us

profile of v2, /device:TPU:1, one launch (start us, length us, event | category | flops | bytes accessed | tf_op | source)
XLA Modules:
  0.0 67.4 jit_solution(8173008896401425357)
XLA Ops:
  1.3 0.0 copy-start
  1.3 0.6 copy-done
  2.0 0.7 %jit_solution_.3.blend_ref = f32[128,128]{1,0:T(8,128)} broadcast(f32[128]{0:T(128)S(1)} %copy-done), dimensions={0} | broadcast | bytes 66048 | tf_op jit(solution)
  2.7 62.6 %shard_map.91 = f32[2,12,64,128]{3,2,1,0:T(8,128)} custom-call(s32[1]{0:T(128)S(6)} %copy.12.offset_ref, s32[1]{0:T(128)S(6)} %copy.11.count_ref, bf16[2,12,64,128]{3,2,1,0:T(8,128)(2,1)} %noisy_ref.1, bf16[12,64,128]{2,1,0:T(8,128)(2,1)} %cond_ref.1, bf16[216,128]{1,0:T(8,128)(2,1)} %bitcast.3, bf16[9,128,128]{2,1,0:T(8,128)(2,1)} %bitcast.2, ...), custom_call_target="tpu_custom_call" | custom-call | flops 24000000000 | bytes 4000000 | tf_op jit(solution)/shard_map/pallas_call | solution.py:478
  65.3 2.1 %copy.13 = f32[2,12,64,128]{3,2,1,0:T(8,128)} copy(f32[2,12,64,128]{3,2,1,0:T(8,128)} %shard_map.91) | data formatting | bytes 1572864
Async XLA Ops:
  1.3 0.7 copy-start

commit v3 on v2

--- a/solution.py
+++ b/solution.py
@@ -3,7 +3,6 @@
 
 import jax
 import jax.numpy as jnp
-import numpy as np
 from jax import lax
 from jax.experimental import pallas as pl
 from jax.experimental.pallas import tpu as pltpu
@@ -74,20 +73,20 @@
     w_mid_ref,
     w_out_ref,
     mod_ref,
-    blend_ref,
     out_ref,
     own_x,
     own_k,
     side_x,
     side_k,
-    plane_send,
-    plane_side,
+    info,
+    info_side,
     term_send,
     term_side,
     step_send,
     step_side,
-    planes_mid,
     term_mid,
+    arrived,
+    blend,
     source,
     stacked,
     ring1,
@@ -143,21 +142,27 @@
         both(m, lambda side: (noisy_ref.at[m], side_x.at[side, m])) for m in range(2)
     ]
     send_k = both(2, lambda side: (cond_ref, side_k.at[side]))
-    send_plane = both(3, lambda side: (plane_send.at[side], plane_side.at[side]))
-    send_term = [
-        both(4 + m, lambda side: (term_send.at[side, m], term_side.at[side, m]))
-        for m in range(2)
-    ]
-    send_step = [
-        both(6 + m, lambda side: (step_send.at[side, m], step_side.at[side, m]))
-        for m in range(2)
-    ]
-
+    send_info = both(3, lambda side: (info, info_side.at[side]))
+
+    def term_copies(m, part):
+        levels = both(
+            4 + 2 * m + part,
+            lambda side: (term_send.at[side, m, part], term_side.at[side, m, part]),
+        )
+        steps = both(
+            8 + 2 * m + part,
+            lambda side: (step_send.at[side, m, part], step_side.at[side, m, part]),
+        )
+        return levels, steps
+
+    send_term = [[term_copies(m, part) for part in range(2)] for m in range(2)]
+
+    offset, count = offset_ref[0], count_ref[0]
+    info[0], info[1] = offset, count
     pl.semaphore_wait(barrier, 2)
-    for copy in send_x[0] + send_k:
+    for copy in send_x[0] + send_k + send_info:
         copy.start()
 
-    offset, count = offset_ref[0], count_ref[0]
     active = [core * 2 + m < count for m in range(2)]
     odd = offset & 1
     even = offset - odd
@@ -222,41 +227,36 @@
             deviation = jnp.where(keep, deviation, 0.0)
         return jnp.sum(deviation, axis=0), jnp.sum(deviation * deviation, axis=0)
 
-    def own_conv(m):
-        def step(i, stats):
-            columns = []
-            for ci in range(4):
-                part = stacked[ci % 2, pl.ds(i * OWN_STEP + ci // 2, OWN_STEP)]
-                columns.append(part.reshape(OWN_STEP * H, F))
-            lhs = jnp.concatenate(columns, axis=1)
-            acc = jnp.dot(lhs, (w1, w1b)[m][...], preferred_element_type=f32)
-            total = squares = jnp.zeros((8, F), f32)
-            for p in range(2):
-                half = acc[:, p * F : (p + 1) * F]
-                feats[p, pl.ds(m * OWN + i * OWN_STEP, OWN_STEP)] = half.reshape(
-                    OWN_STEP, H, F
-                )
-                more = deviations(stats, half)
-                total, squares = total + more[0], squares + more[1]
-            return merge(stats, 2.0 * OWN_STEP * H, total, squares)
-
-        zero = jnp.zeros((8, F), f32)
-        return lax.fori_loop(0, OWN // OWN_STEP, step, (zero, zero, zero))
-
-    own_stats = [own_conv(m) for m in range(2)]
-
-    terms[0, pl.ds(0, BW)] = jnp.zeros((BW, H), f32)
-    terms[0, pl.ds(BW, PW)] = blend_ref[...]
-    terms[0, pl.ds(BW + PW, BW)] = jnp.zeros((BW, H), f32)
-    for block, target in ((0, plane_send.at[1]), (1, planes_mid), (2, plane_send.at[0])):
-        plane = terms[0, pl.ds(BW + BW * block - offset, BW)]
-        target[0] = plane
-        for m in range(2):
-            target[1 + m] = jnp.where(active[m], plane, 0.0)
-    for copy in send_plane:
-        copy.start()
-    terms[:, pl.ds(0, BW)] = jnp.zeros((C, BW, H), f32)
-    terms[:, pl.ds(BW + PW, BW)] = jnp.zeros((C, BW, H), f32)
+    def own_conv(m, i, stats):
+        columns = []
+        for ci in range(4):
+            part = stacked[ci % 2, pl.ds(i * OWN_STEP + ci // 2, OWN_STEP)]
+            columns.append(part.reshape(OWN_STEP * H, F))
+        lhs = jnp.concatenate(columns, axis=1)
+        acc = jnp.dot(lhs, (w1, w1b)[m][...], preferred_element_type=f32)
+        total = squares = jnp.zeros((8, F), f32)
+        for p in range(2):
+            half = acc[:, p * F : (p + 1) * F]
+            feats[p, pl.ds(m * OWN + i * OWN_STEP, OWN_STEP)] = half.reshape(OWN_STEP, H, F)
+            more = deviations(stats, half)
+            total, squares = total + more[0], squares + more[1]
+        return merge(stats, 2.0 * OWN_STEP * H, total, squares)
+
+    zero = jnp.zeros((8, F), f32)
+    own_steps = OWN // OWN_STEP
+    own_stats = lax.fori_loop(0, own_steps, functools.partial(own_conv, 0), (zero, zero, zero))
+
+    place = lax.broadcasted_iota(jnp.int32, (PW, H), 0).astype(f32)
+    angle = jnp.square((place + 0.5) * (math.pi / PW) - math.pi / 2)
+    wave = jnp.zeros((PW, H), f32)
+    for n in range(8, -1, -1):
+        wave = wave * angle + (-1.0) ** n / math.factorial(2 * n)
+    blend[pl.ds(0, BW)] = jnp.zeros((BW, H), f32)
+    blend[pl.ds(BW, PW)] = 0.1 + wave * wave
+    blend[pl.ds(BW + PW, BW)] = jnp.zeros((BW, H), f32)
+    for c in range(C):
+        arrived[0, c, pl.ds(BW, BW)] = jnp.zeros((BW, H), f32)
+        arrived[1, c, pl.ds(0, BW)] = jnp.zeros((BW, H), f32)
 
     out_rows = jnp.concatenate([w_out_ref[...].astype(f32), jnp.zeros((4, F), f32)], axis=0)
     spread_rows = jnp.broadcast_to(out_rows[:, None, :], (16, 8, F)).reshape(F, F).T
@@ -271,7 +271,9 @@
                 block = rolled[a * 3 + b] if 0 <= a < 3 else zeros128
                 w2[pl.ds((b * 4 + ci) * 128, 128), pl.ds(p * 128, 128)] = block
 
-    rings1, rings2 = (ring1, ring1b), (ring2, ring2b)
+    rings1 = (ring1, ring1b)
+    terms[:, pl.ds(0, BW)] = jnp.zeros((C, BW, H), f32)
+    terms[:, pl.ds(BW + PW, BW)] = jnp.zeros((C, BW, H), f32)
 
     def rest_stack(g):
         for t in range(2 * REST_STEP + 4):
@@ -364,57 +366,57 @@
         fill(m, affine, 2 * i + 2, ring2, ring2b)
         return stats, affine
 
-    def out_step(i, carry):
-        scale, bias = carry
-        for sub in range(2):
-            base = i * 32 + sub * 16
-            columns = []
-            for k in range(8):
-                rows = []
-                for g in range(4):
-                    u = sums[k % 2, base + g * 4 + k // 2] * scale + bias
-                    rows.append(silu_of_twice(u).astype(bf16))
-                columns.append(jnp.concatenate(rows, axis=0))
-            result = jnp.dot(
-                jnp.concatenate(columns, axis=1), w3[...], preferred_element_type=f32
-            )
+    def out_columns(part, affine):
+        columns = []
+        for k in range(8):
+            rows = []
             for g in range(4):
-                flipped = result[g * H : (g + 1) * H].T.reshape(16, 8, H)[:C]
-                at = 2 * base + g * 8
-                weight = blend_ref[pl.ds(at, 8)] * (-step_factor * output_scale)
-                terms[:, pl.ds(BW + at, 8)] = flipped * weight
-        return carry
-
-    for copy in send_k:
-        copy.wait_recv()
-    put_cond(side_k.at[0], 0)
-    put_cond(side_k.at[1], 2)
-
-    for m in range(2):
-        if m == 1:
-            put_state(own_x.at[m], 0, 1)
-        for copy in send_x[m]:
-            copy.wait_recv()
-        if m == 0:
-            for copy in send_x[1]:
-                copy.start()
+                u = sums[k % 2, part * 16 + g * 4 + k // 2] * affine[0] + affine[1]
+                rows.append(silu_of_twice(u).astype(bf16))
+            columns.append(jnp.concatenate(rows, axis=0))
+        result = jnp.dot(jnp.concatenate(columns, axis=1), w3[...], preferred_element_type=f32)
+        for g in range(4):
+            flipped = result[g * H : (g + 1) * H].T.reshape(16, 8, H)[:C]
+            at = 32 * part + g * 8
+            weight = blend[pl.ds(BW + at, 8)] * (-step_factor * output_scale)
+            terms[:, pl.ds(BW + at, 8)] = flipped * weight
+
+    routes = ((1, 0), (1, 1), (0, 1), (0, 0))
+
+    def send_columns(part, m):
+        side, half = routes[part]
+        values = [terms[c, pl.ds(BW + 32 * part, 32)].reshape(4, 8, H) for c in range(C)]
+        largest = jnp.full((8, H), 1e-30, f32)
+        for value in values:
+            largest = jnp.maximum(largest, jnp.max(jnp.abs(value), axis=0))
+        step_send[side, m, half] = jnp.where(active[m], largest * (1.0 / LEVELS), 0.0)
+        inverse = LEVELS / largest
+        for c in range(C):
+            levels = jnp.round(values[c] * inverse).astype(jnp.int32)
+            term_send[side, m, half, c] = levels.reshape(32, H).astype(jnp.int16)
+        for copies in send_term[m][half]:
+            copies[side].start()
+
+    def keep_own(m):
+        for c in range(C):
+            part = terms[c, pl.ds(2 * BW - offset, BW)]
+            term_mid[m, c] = jnp.where(active[m], part, 0.0)
+
+    def put_sides(m):
         put_state(side_x.at[0, m], 0, 0)
         put_state(side_x.at[1, m], 0, 2)
-        stats = own_stats[m]
-        rest_stack(0)
-        for g in range(3):
-            if g < 2:
-                rest_stack(g + 1)
-            stats = rest_conv(g, m, stats)
+
+    def hidden_affine(stats):
         scale, bias = norm_affine(stats[1], stats[2])
         gain = 1.0 + mod_ref[0:1]
-        scale, bias = scale * gain * 0.5, (bias * gain + mod_ref[1:2]) * 0.5
-        affine = scale[0:1], bias[0:1]
+        return (scale * gain * 0.5)[0:1], ((bias * gain + mod_ref[1:2]) * 0.5)[0:1]
+
+    def middle(m, stats):
+        affine = hidden_affine(stats)
         for b in range(3):
             ring2[b, 0, 0] = zeros128
         put_hidden(m, affine, jnp.int32(0), [(ring2, 1)])
         fill(m, affine, 0, ring2, ring2b)
-        zero = jnp.zeros((8, F), f32)
         (stats, _) = lax.fori_loop(
             0,
             BW // PAIRS // 2,
@@ -422,55 +424,89 @@
             ((zero, stats[1], zero), affine),
         )
         scale, bias = norm_affine(stats[1], stats[2])
-        lax.fori_loop(0, 2, out_step, (scale[0:1] * 0.5, bias[0:1] * 0.5))
-        for block, side in ((0, 1), (2, 0)):
-            largest = jnp.full((8, H), 1e-30, f32)
-            for c in range(C):
-                part = terms[c, pl.ds(BW + BW * block - offset, BW)]
-                part = jnp.max(jnp.abs(part).reshape(8, 8, H), axis=0)
-                largest = jnp.maximum(largest, part)
-            step_send[side, m] = jnp.where(active[m], largest * (1.0 / LEVELS), 0.0)
-            inverse = LEVELS / largest
-            for c in range(C):
-                part = terms[c, pl.ds(BW + BW * block - offset, BW)].reshape(8, 8, H)
-                levels = jnp.round(part * inverse).astype(jnp.int32)
-                term_send[side, m, c] = levels.reshape(BW, H).astype(jnp.int16)
-            send_term[m][side].start()
-            send_step[m][side].start()
-        for c in range(C):
-            part = terms[c, pl.ds(2 * BW - offset, BW)]
-            term_mid[m, c] = jnp.where(active[m], part, 0.0)
-
-    for copy in send_plane:
+        return scale[0:1] * 0.5, bias[0:1] * 0.5
+
+    for copy in send_k:
         copy.wait_recv()
-    planes = [planes_mid[q] + plane_side[0, q] + plane_side[1, q] for q in range(3)]
-    inverse = 1.0 / planes[0]
+    put_cond(side_k.at[0], 0)
+    put_cond(side_k.at[1], 2)
+    for copy in send_x[0]:
+        copy.wait_recv()
+    for copy in send_x[1]:
+        copy.start()
+    put_sides(0)
+
+    stats, other = own_stats, (zero, zero, zero)
+    rest_stack(0)
+    for g in range(3):
+        other = own_conv(1, g, other)
+        if g < 2:
+            rest_stack(g + 1)
+        stats = rest_conv(g, 0, stats)
+    affine = middle(0, stats)
+
+    for copy in send_x[1] + send_info:
+        copy.wait_recv()
+    put_state(own_x.at[1], 0, 1)
+    put_sides(1)
+    stats = other
+    rest_stack(0)
+    out_columns(0, affine)
+    for g in range(3):
+        if g < 2:
+            rest_stack(g + 1)
+        stats = rest_conv(g, 1, stats)
+        out_columns(g + 1, affine)
+    for part in range(4):
+        send_columns(part, 0)
+    keep_own(0)
+
+    affine = middle(1, stats)
+    for part in (0, 3, 1, 2):
+        out_columns(part, affine)
+        send_columns(part, 1)
+    keep_own(1)
+
+    shifts = (offset, info_side[0, 0], info_side[1, 0])
+    starts = (2 * BW - shifts[0], BW + PW - shifts[1], BW - shifts[2])
+    members = (count, info_side[0, 1], info_side[1, 1])
+    planes = [blend[pl.ds(start, BW)] for start in starts]
+    inverse = 1.0 / (planes[0] + planes[1] + planes[2])
     for m in range(2):
-        for copy in send_step[m] + send_term[m]:
-            copy.wait_recv()
-        factor = planes[1 + m] * (step_factor * (1.0 - skip_scale))
-        steps = [step_side[side, m] for side in range(2)]
+        factor = jnp.zeros((BW, H), f32)
+        for plane, number in zip(planes, members):
+            factor = factor + jnp.where(core * 2 + m < number, plane, 0.0)
+        factor = factor * (step_factor * (1.0 - skip_scale))
+        for half in range(2):
+            for copies in send_term[m][half]:
+                for copy in copies:
+                    copy.wait_recv()
+            for side in range(2):
+                step = step_side[side, m, half]
+                at = BW + 32 * half if side == 1 else 32 * (1 - half)
+                for c in range(C):
+                    levels = term_side[side, m, half, c].astype(jnp.int32).astype(f32)
+                    values = (levels.reshape(4, 8, H) * step).reshape(32, H)
+                    arrived[side, c, pl.ds(at, 32)] = values
         for c in range(C):
             x = own_x[m, c].astype(f32)
             numerator = term_mid[m, c]
             for side in range(2):
-                levels = term_side[side, m, c].astype(jnp.int32).astype(f32)
-                numerator = numerator + (levels.reshape(8, 8, H) * steps[side]).reshape(BW, H)
+                numerator = numerator + arrived[side, c, pl.ds(BW - shifts[1 + side], BW)]
             out_ref[m, c] = x + (x * factor + numerator) * inverse
 
-    sent = send_k + send_plane
+    sent = send_k + send_info
     for m in range(2):
-        sent = sent + send_x[m] + send_term[m] + send_step[m]
+        sent = sent + send_x[m]
+        for half in range(2):
+            for copies in send_term[m][half]:
+                sent = sent + copies
     for copy in sent:
         copy.wait_send()
 
 
 def solution(mesh):
     owners = mesh.shape["owner"]
-    places = (np.arange(PW) + 0.5).astype(np.float32)
-    blend = 0.1 + np.sin(np.float32(math.pi) * places / np.float32(PW)) ** 2
-    blend = np.broadcast_to(blend.astype(np.float32)[:, None], (PW, H))
-
     def on_device(noisy, cond, counts, offsets, w_in, w_mid, w_out, mod):
         smem = pl.BlockSpec(memory_space=pltpu.SMEM)
         vmem = pl.BlockSpec(memory_space=pltpu.VMEM)
@@ -478,21 +514,22 @@
         return pl.pallas_call(
             functools.partial(kernel, owners),
             out_shape=jax.ShapeDtypeStruct((2, C, BW, H), f32),
-            in_specs=[smem, smem, hbm, hbm, vmem, hbm, vmem, vmem, vmem],
+            in_specs=[smem, smem, hbm, hbm, vmem, hbm, vmem, vmem],
             out_specs=vmem,
             scratch_shapes=[
                 pltpu.VMEM((2, C, BW, H), bf16),
                 pltpu.VMEM((C, BW, H), bf16),
                 pltpu.VMEM((2, 2, C, BW, H), bf16),
                 pltpu.VMEM((2, C, BW, H), bf16),
-                pltpu.VMEM((2, 3, BW, H), f32),
-                pltpu.VMEM((2, 3, BW, H), f32),
-                pltpu.VMEM((2, 2, C, BW, H), jnp.int16),
-                pltpu.VMEM((2, 2, C, BW, H), jnp.int16),
-                pltpu.VMEM((2, 2, 8, H), f32),
-                pltpu.VMEM((2, 2, 8, H), f32),
-                pltpu.VMEM((3, BW, H), f32),
+                pltpu.SMEM((2,), jnp.int32),
+                pltpu.SMEM((2, 2), jnp.int32),
+                pltpu.VMEM((2, 2, 2, C, 32, H), jnp.int16),
+                pltpu.VMEM((2, 2, 2, C, 32, H), jnp.int16),
+                pltpu.VMEM((2, 2, 2, 8, H), f32),
+                pltpu.VMEM((2, 2, 2, 8, H), f32),
                 pltpu.VMEM((2, C, BW, H), f32),
+                pltpu.VMEM((2, C, PW, H), f32),
+                pltpu.VMEM((2 * PW, H), f32),
                 pltpu.VMEM((LANES * STRIDE, H), f32),
                 pltpu.VMEM((2, BW // 2, H, F), bf16),
                 pltpu.VMEM((2, REST_STEP + 2, H, F), bf16),
@@ -508,8 +545,8 @@
                 pltpu.VMEM((12 * F, 2 * F), bf16),
                 pltpu.VMEM((8 * F, F), bf16),
                 pltpu.SemaphoreType.DMA((3,)),
-                pltpu.SemaphoreType.DMA((8, 2)),
-                pltpu.SemaphoreType.DMA((8, 2)),
+                pltpu.SemaphoreType.DMA((12, 2)),
+                pltpu.SemaphoreType.DMA((12, 2)),
             ],
             compiler_params=pltpu.CompilerParams(
                 collective_id=0, has_side_effects=True, vmem_limit_bytes=56 * 2**20
@@ -526,7 +563,6 @@
             w_mid.reshape(9, F, F),
             w_out,
             mod,
-            jnp.asarray(blend),
         )
 
     placed = (

time: 67.9 us -> 65.2 us (0.960)
  local copies, waits for them, and re-layouts: 3.45 us -> 2.09 us
  Pallas kernels: 62.6 us -> 61.7 us
    pallas_call x1, Pallas kernels: 62.6 us -> 61.7 us  [on_device(): pl.pallas_call(functools.partial(kernel, owners), out_shape=jax.ShapeDtyp...]
    another operation x1 -> x0, local copies, waits for them, and re-layouts: 0.71 us -> none
    unnamed x3 -> x1, local copies, waits for them, and re-layouts: 2.74 us -> 2.09 us
where the time goes in v3:
time: 65.2 us; the launch traced here: 65 us
  Pallas kernels  61.7 us (95%)
  local copies, waits for them, and re-layouts  2.09 us (3%)
  between operations  1.31 us (2%)
    pallas_call x1, Pallas kernels, on_device(): pl.pallas_call(functools.partial(kernel, owners), out_shape=jax.ShapeDtyp...  61.7 us
    unnamed x1, local copies, waits for them, and re-layouts  2.09 us

profile of v3, /device:TPU:1, one launch (start us, length us, event | category | flops | bytes accessed | tf_op | source)
XLA Modules:
  0.0 65.0 jit_solution(9945309921784169113)
XLA Ops:
  1.3 61.7 %shard_map.82 = f32[2,12,64,128]{3,2,1,0:T(8,128)} custom-call(s32[1]{0:T(128)S(6)} %copy.11.offset_ref, s32[1]{0:T(128)S(6)} %copy.10.count_ref, bf16[2,12,64,128]{3,2,1,0:T(8,128)(2,1)} %noisy_ref.1, bf16[12,64,128]{2,1,0:T(8,128)(2,1)} %cond_ref.1, bf16[216,128]{1,0:T(8,128)(2,1)} %bitcast.3, bf16[9,128,128]{2,1,0:T(8,128)(2,1)} %bitcast.2, ...), custom_call_target="tpu_custom_call" | custom-call | flops 24000000000 | bytes 4000000 | tf_op jit(solution)/shard_map/pallas_call | solution.py:514
  63.0 2.1 %copy.12 = f32[2,12,64,128]{3,2,1,0:T(8,128)} copy(f32[2,12,64,128]{3,2,1,0:T(8,128)} %shard_map.82) | data formatting | bytes 1572864

commit v4 on v3

--- a/solution.py
+++ b/solution.py
@@ -113,6 +113,7 @@
     barrier = pltpu.get_barrier_semaphore()
     for neighbour in (left, right):
         pl.semaphore_signal(barrier, inc=1, device_id=(neighbour, core), device_id_type=MESH)
+    pl.semaphore_signal(barrier, inc=1, device_id=(me, 1 - core), device_id_type=MESH)
 
     local = [
         pltpu.make_async_copy(noisy_ref, own_x, local_sem.at[0]),
@@ -122,7 +123,7 @@
     for copy in local:
         copy.start()
 
-    def both(kind, make):
+    def both(kind, make, across=False):
         copies = []
         for side in range(2):
             source_ref, target_ref = make(side)
@@ -132,7 +133,7 @@
                     dst_ref=target_ref,
                     send_sem=send_sem.at[kind, side],
                     recv_sem=recv_sem.at[kind, side],
-                    device_id=(targets[side], core),
+                    device_id=(me, 1 - core) if across else (targets[side], core),
                     device_id_type=MESH,
                 )
             )
@@ -141,7 +142,11 @@
     send_x = [
         both(m, lambda side: (noisy_ref.at[m], side_x.at[side, m])) for m in range(2)
     ]
-    send_k = both(2, lambda side: (cond_ref, side_k.at[side]))
+    half_k = pl.ds(core * (C // 2), C // 2)
+    send_k = both(2, lambda side: (cond_ref.at[half_k], side_k.at[side, half_k]))
+    share_k = both(
+        12, lambda side: (side_k.at[side, half_k], side_k.at[side, half_k]), across=True
+    )
     send_info = both(3, lambda side: (info, info_side.at[side]))
 
     def term_copies(m, part):
@@ -159,8 +164,8 @@
 
     offset, count = offset_ref[0], count_ref[0]
     info[0], info[1] = offset, count
-    pl.semaphore_wait(barrier, 2)
-    for copy in send_x[0] + send_k + send_info:
+    pl.semaphore_wait(barrier, 3)
+    for copy in send_k + send_x[0] + send_info:
         copy.start()
 
     active = [core * 2 + m < count for m in range(2)]
@@ -220,6 +225,9 @@
         return carry
 
     lax.fori_loop(0, 4, own_stack_step, 0)
+    for copy, share in zip(send_k, share_k):
+        copy.wait_recv()
+        share.start()
 
     def deviations(stats, values, keep=None):
         deviation = values.reshape(-1, 8, F) - stats[1]
@@ -426,7 +434,7 @@
         scale, bias = norm_affine(stats[1], stats[2])
         return scale[0:1] * 0.5, bias[0:1] * 0.5
 
-    for copy in send_k:
+    for copy in share_k:
         copy.wait_recv()
     put_cond(side_k.at[0], 0)
     put_cond(side_k.at[1], 2)
@@ -495,7 +503,7 @@
                 numerator = numerator + arrived[side, c, pl.ds(BW - shifts[1 + side], BW)]
             out_ref[m, c] = x + (x * factor + numerator) * inverse
 
-    sent = send_k + send_info
+    sent = send_k + share_k + send_info
     for m in range(2):
         sent = sent + send_x[m]
         for half in range(2):
@@ -545,8 +553,8 @@
                 pltpu.VMEM((12 * F, 2 * F), bf16),
                 pltpu.VMEM((8 * F, F), bf16),
                 pltpu.SemaphoreType.DMA((3,)),
-                pltpu.SemaphoreType.DMA((12, 2)),
-                pltpu.SemaphoreType.DMA((12, 2)),
+                pltpu.SemaphoreType.DMA((13, 2)),
+                pltpu.SemaphoreType.DMA((13, 2)),
             ],
             compiler_params=pltpu.CompilerParams(
                 collective_id=0, has_side_effects=True, vmem_limit_bytes=56 * 2**20

time: 65.2 us -> 63.1 us (0.968)
  Pallas kernels: 61.7 us -> 59.5 us
    pallas_call x1, Pallas kernels: 61.7 us -> 59.5 us  [on_device(): pl.pallas_call(functools.partial(kernel, owners), out_shape=jax.ShapeDtyp...]
where the time goes in v4:
time: 63.1 us; the launch traced here: 62.9 us
  Pallas kernels  59.5 us (94%)
  local copies, waits for them, and re-layouts  2.09 us (3%)
  between operations  1.31 us (2%)
    pallas_call x1, Pallas kernels, on_device(): pl.pallas_call(functools.partial(kernel, owners), out_shape=jax.ShapeDtyp...  59.5 us
    unnamed x1, local copies, waits for them, and re-layouts  2.09 us

profile of v4, /device:TPU:1, one launch (start us, length us, event | category | flops | bytes accessed | tf_op | source)
XLA Modules:
  0.0 62.9 jit_solution(14336311231465892399)
XLA Ops:
  1.3 59.5 %shard_map.82 = f32[2,12,64,128]{3,2,1,0:T(8,128)} custom-call(s32[1]{0:T(128)S(6)} %copy.11.offset_ref, s32[1]{0:T(128)S(6)} %copy.10.count_ref, bf16[2,12,64,128]{3,2,1,0:T(8,128)(2,1)} %noisy_ref.1, bf16[12,64,128]{2,1,0:T(8,128)(2,1)} %cond_ref.1, bf16[216,128]{1,0:T(8,128)(2,1)} %bitcast.3, bf16[9,128,128]{2,1,0:T(8,128)(2,1)} %bitcast.2, ...), custom_call_target="tpu_custom_call" | custom-call | flops 24000000000 | bytes 4000000 | tf_op jit(solution)/shard_map/pallas_call | solution.py:522
  60.8 2.1 %copy.12 = f32[2,12,64,128]{3,2,1,0:T(8,128)} copy(f32[2,12,64,128]{3,2,1,0:T(8,128)} %shard_map.82) | data formatting | bytes 1572864
